TPU v7x, 32 devices: a whole 2x2x4 slice. The times are simulated.
32 devices in a mesh: dp: 8 (over z, x), zero: 4 (over y, core).
Axes of the slice: x: 2, y: 2, z: 4, core: 2. Of those that a mesh axis runs over, the one named last changes fastest.
Arguments:
- tokens: bfloat16 [16384, 256], P(('dp', 'zero')), may hold values from -6 to 6
- cotangent: bfloat16 [16384, 256], P(('dp', 'zero')), may hold values from -6 to 6
- lengths: int32 [32, 2], P(('dp', 'zero')), may hold values from 0 to 512, as said below
- qkv_weight: float32 [256, 768], P('zero'), may hold values from -0.375 to 0.375
- out_weight: float32 [256, 256], P('zero'), may hold values from -3 to 3
- up_weight: float32 [256, 1024], P('zero'), may hold values from -0.375 to 0.375
- down_weight: float32 [1024, 256], P('zero'), may hold values from -0.1875 to 0.1875
- vectors: float32 [3328], P('zero'), may hold values from -0.8 to 1.4, as said below
- qkv_first: float32 [256, 768], P('zero'), may hold values from -24 to 24
- out_first: float32 [256, 256], P('zero'), may hold values from -24 to 24
- up_first: float32 [256, 1024], P('zero'), may hold values from -24 to 24
- down_first: float32 [1024, 256], P('zero'), may hold values from -24 to 24
- vectors_first: float32 [3328], P('zero'), may hold values from -80 to 80
- qkv_second: float32 [256, 768], P('zero'), may hold values from 32.768 to 491.52
- out_second: float32 [256, 256], P('zero'), may hold values from 32.768 to 491.52
- up_second: float32 [256, 1024], P('zero'), may hold values from 32.768 to 491.52
- down_second: float32 [1024, 256], P('zero'), may hold values from 32.768 to 491.52
- vectors_second: float32 [3328], P('zero'), may hold values from 327.68 to 4915.2
Outputs:
- activations: bfloat16 [16384, 256], P(('dp', 'zero'))
- input_grad: bfloat16 [16384, 256], P(('dp', 'zero'))
- qkv_updated: float32 [256, 768], P('zero')
- out_updated: float32 [256, 256], P('zero')
- up_updated: float32 [256, 1024], P('zero')
- down_updated: float32 [1024, 256], P('zero')
- vectors_updated: float32 [3328], P('zero')
- qkv_momentum: float32 [256, 768], P('zero')
- out_momentum: float32 [256, 256], P('zero')
- up_momentum: float32 [256, 1024], P('zero')
- down_momentum: float32 [1024, 256], P('zero')
- vectors_momentum: float32 [3328], P('zero')
- qkv_variance: float32 [256, 768], P('zero')
- out_variance: float32 [256, 256], P('zero')
- up_variance: float32 [256, 1024], P('zero')
- down_variance: float32 [1024, 256], P('zero')
- vectors_variance: float32 [3328], P('zero')
Inputs may be any that keep to these rules, and one draw needn't show every extreme that they name: Row b lists the lengths of the two sequences of buffer b; a row sums to between 256 and 512, its first entry is at least half of its sum, and some buffer holds one sequence of 512 tokens and an empty second one. `vectors`: g1 and g2 lie near one, the biases near zero.
All inputs are finite; a program needn't handle non-finite values.
Results may differ from a plain program's by a relative error of at most 0.0055.
The roundings to bfloat16 on the way count: a program that leaves them out, or rounds other values in their place, can miss the bound.
Values may be sent and summed in bfloat16 or wider, within the bound.
A program may use at most 64 MiB of HBM per device.

v0:
```python
import jax
import jax.numpy as jnp
from jax import lax
from jax.sharding import PartitionSpec as P

HEADS = 8
HEAD_DIM = 32
ROT = 8
STEP = 5


NORM_EPS = 1e-05
BETA_ONE = 0.9
BETA_TWO = 0.95
ADAM_EPS = 1e-08
DECAY = 0.01
RATE_MATRIX = 0.06
RATE_OUTPUT = 0.3
RATE_VECTOR = 0.5
NEGATIVE = -1e30


def layout(pair, count):
    first = pair[0]
    total = pair[0] + pair[1]
    index = jnp.arange(count, dtype=jnp.int32)
    segment = (index >= first).astype(jnp.int32) + (index >= total).astype(jnp.int32)
    start = jnp.where(segment == 0, 0, jnp.where(segment == 1, first, total))
    position = (index - start).astype(jnp.float32)
    live = (index < total).astype(jnp.float32)
    return (segment, position, live)


def unpack(vector, width, hidden):
    sizes_list = (width, width, width, width, 3 * width, width, hidden, width)
    pieces = []
    begin = 0
    for length in sizes_list:
        pieces.append(vector[begin : begin + length])
        begin = begin + length
    return pieces


def normalize(rows):
    centered = rows - jnp.mean(rows, axis=1, keepdims=True)
    return centered * lax.rsqrt(jnp.mean(centered * centered, axis=1, keepdims=True) + NORM_EPS)


def both_norms(rows, gain_one, bias_one, gain_two, bias_two):
    plain = normalize(rows)
    return (plain * gain_one + bias_one, plain * gain_two + bias_two)


def gelu_exact(values):
    return jax.nn.gelu(values, approximate=False)


def rotate(lines, position, sign):
    count = lines.shape[0]
    half = ROT // 2
    shaped = lines.reshape(count, -1, HEAD_DIM)
    freq = 1.0 / 10000.0 ** (jnp.arange(half, dtype=jnp.float32) * 2.0 / ROT)
    angle = position[:, None] * freq[None, :]
    cosine = jnp.cos(angle)[:, None, :]
    sine = sign * jnp.sin(angle)[:, None, :]
    lower = shaped[:, :, :half]
    upper = shaped[:, :, half:ROT]
    turned = jnp.concatenate(
        [lower * cosine - upper * sine, upper * cosine + lower * sine, shaped[:, :, ROT:]], axis=2
    )
    return turned.reshape(count, -1)


def block_scores(query, key_heads, segment, begin, block):
    count = key_heads.shape[0]
    rows = query.reshape(block, HEADS, HEAD_DIM)
    row_index = begin + jnp.arange(block, dtype=jnp.int32)
    key_index = jnp.arange(count, dtype=jnp.int32)
    allowed = (segment[:, None] == segment[None, :]) & (key_index[None, :] <= row_index[:, None])
    scores = jnp.einsum(
        "qhd,khd->hqk", rows, key_heads, preferred_element_type=jnp.float32
    ) * HEAD_DIM ** (-0.5)
    return (rows, jnp.where(allowed[None], scores, NEGATIVE))


def attend_forward(query, keys, values, segment, block):
    count = query.shape[0]
    key_heads = keys.reshape(count, HEADS, HEAD_DIM)
    value_heads = values.reshape(count, HEADS, HEAD_DIM)

    def one_block(number):
        rows, scores = block_scores(query, key_heads, segment, number * block, block)
        peak = jnp.max(scores, axis=2, keepdims=True)
        raised = jnp.exp(scores - peak)
        total = jnp.sum(raised, axis=2, keepdims=True)
        weights = (raised / total).astype(jnp.bfloat16)
        mixed = jnp.einsum("hqk,khd->qhd", weights, value_heads, preferred_element_type=jnp.float32)
        return (mixed.reshape(block, -1), (peak + jnp.log(total))[:, :, 0])

    mixed, logsum = lax.map(one_block, jnp.arange(count // block, dtype=jnp.int32))
    return (mixed.reshape(count, -1), logsum)


def attend_backward(query, keys, values, mixed_grad, segment, logsum, block):
    count = query.shape[0]
    scale = HEAD_DIM ** (-0.5)
    key_heads = keys.reshape(count, HEADS, HEAD_DIM)
    value_heads = values.reshape(count, HEADS, HEAD_DIM)

    def one_block(carry, number):
        key_grad, value_grad = carry
        begin = number * block
        rows, scores = block_scores(query, key_heads, segment, begin, block)
        row_grad = mixed_grad.reshape(block, HEADS, HEAD_DIM)
        chances = jnp.exp(scores - logsum[number][:, :, None])
        weights = chances.astype(jnp.bfloat16)
        inner = jnp.einsum(
            "qhd,khd->hqk", row_grad, value_heads, preferred_element_type=jnp.float32
        )
        slope = (chances * (inner - jnp.sum(inner * chances, axis=2, keepdims=True))).astype(
            jnp.bfloat16
        )
        query_grad = (
            jnp.einsum("hqk,khd->qhd", slope, key_heads, preferred_element_type=jnp.float32) * scale
        )
        key_grad = (
            key_grad
            + jnp.einsum("hqk,qhd->khd", slope, rows, preferred_element_type=jnp.float32) * scale
        )
        value_grad = value_grad + jnp.einsum(
            "hqk,qhd->khd", weights, row_grad, preferred_element_type=jnp.float32
        )
        return ((key_grad, value_grad), query_grad.reshape(block, -1))

    zeros = jnp.zeros((count, HEADS, HEAD_DIM), jnp.float32)
    (key_grad, value_grad), query_grad = lax.scan(
        one_block, (zeros, zeros), jnp.arange(count // block, dtype=jnp.int32)
    )
    return (
        query_grad.reshape(count, -1),
        key_grad.reshape(count, -1),
        value_grad.reshape(count, -1),
    )


def adamw(master, first, second, grad, rate):
    momentum = BETA_ONE * first + (1.0 - BETA_ONE) * grad
    variance = BETA_TWO * second + (1.0 - BETA_TWO) * grad * grad
    direction = (
        momentum / (1.0 - BETA_ONE**STEP) / (jnp.sqrt(variance / (1.0 - BETA_TWO**STEP)) + ADAM_EPS)
    )
    return (master - rate * (direction + DECAY * master), momentum, variance)


def on_device(
    tokens,
    cotangent,
    lengths,
    qkv_weight,
    out_weight,
    up_weight,
    down_weight,
    vectors,
    qkv_first,
    out_first,
    up_first,
    down_first,
    vectors_first,
    qkv_second,
    out_second,
    up_second,
    down_second,
    vectors_second,
):
    qkv_full, out_full, up_full, down_full, vector_full = (
        lax.all_gather(qkv_weight.astype(jnp.bfloat16), "zero", axis=0, tiled=True),
        lax.all_gather(out_weight.astype(jnp.bfloat16), "zero", axis=0, tiled=True),
        lax.all_gather(up_weight.astype(jnp.bfloat16), "zero", axis=0, tiled=True),
        lax.all_gather(down_weight.astype(jnp.bfloat16), "zero", axis=0, tiled=True),
        lax.all_gather(vectors.astype(jnp.bfloat16), "zero", axis=0, tiled=True),
    )
    count = tokens.shape[0]
    width = tokens.shape[1]
    hidden = up_full.shape[1]
    block = min(512, count)
    segment, position, live = layout(lengths[0], count)
    gain_one, bias_one, gain_two, bias_two, qkv_bias, out_bias, up_bias, down_bias = unpack(
        vector_full.astype(jnp.float32), width, hidden
    )
    rows = tokens.astype(jnp.float32)
    (norm_one, norm_two), norm_pull = jax.vjp(
        both_norms, rows, gain_one, bias_one, gain_two, bias_two
    )
    hidden_one = norm_one.astype(jnp.bfloat16)
    hidden_two = norm_two.astype(jnp.bfloat16)
    lines = jnp.dot(hidden_one, qkv_full, preferred_element_type=jnp.float32) + qkv_bias
    turned = rotate(lines[:, : 2 * width], position, 1.0)
    query = turned[:, :width].astype(jnp.bfloat16)
    keys = turned[:, width:].astype(jnp.bfloat16)
    values = lines[:, 2 * width :].astype(jnp.bfloat16)
    mixed, logsum = attend_forward(query, keys, values, segment, block)
    mixed_low = mixed.astype(jnp.bfloat16)
    attn_out = jnp.dot(mixed_low, out_full, preferred_element_type=jnp.float32) + out_bias
    up_lines = jnp.dot(hidden_two, up_full, preferred_element_type=jnp.float32) + up_bias
    active, gelu_pull = jax.vjp(gelu_exact, up_lines)
    active_low = active.astype(jnp.bfloat16)
    mlp_out = jnp.dot(active_low, down_full, preferred_element_type=jnp.float32) + down_bias
    activations = (live[:, None] * (rows + attn_out + mlp_out)).astype(jnp.bfloat16)
    back = cotangent.astype(jnp.float32) * live[:, None]
    back_low = back.astype(jnp.bfloat16)
    back_total = jnp.sum(back, axis=0)
    grad_out_w = jnp.einsum("td,te->de", mixed_low, back_low, preferred_element_type=jnp.float32)
    grad_down_w = jnp.einsum("tf,te->fe", active_low, back_low, preferred_element_type=jnp.float32)
    mixed_grad = jnp.einsum(
        "te,de->td", back_low, out_full, preferred_element_type=jnp.float32
    ).astype(jnp.bfloat16)
    active_grad = jnp.einsum("te,fe->tf", back_low, down_full, preferred_element_type=jnp.float32)
    up_grad = gelu_pull(active_grad)[0].astype(jnp.bfloat16)
    grad_up_w = jnp.einsum("td,tf->df", hidden_two, up_grad, preferred_element_type=jnp.float32)
    two_grad = jnp.einsum("tf,df->td", up_grad, up_full, preferred_element_type=jnp.float32)
    query_grad, key_grad, value_grad = attend_backward(
        query, keys, values, mixed_grad, segment, logsum, block
    )
    turned_grad = rotate(jnp.concatenate([query_grad, key_grad], axis=1), position, -1.0)
    lines_grad = jnp.concatenate([turned_grad, value_grad], axis=1).astype(jnp.bfloat16)
    grad_qkv_w = jnp.einsum("td,te->de", hidden_one, lines_grad, preferred_element_type=jnp.float32)
    one_grad = jnp.einsum("te,de->td", lines_grad, qkv_full, preferred_element_type=jnp.float32)
    rows_grad, gain_one_grad, bias_one_grad, gain_two_grad, bias_two_grad = norm_pull(
        (one_grad, two_grad)
    )
    input_grad = (rows_grad + back).astype(jnp.bfloat16)
    vector_grad = jnp.concatenate(
        [
            gain_one_grad,
            bias_one_grad,
            gain_two_grad,
            bias_two_grad,
            jnp.sum(lines_grad.astype(jnp.float32), axis=0),
            back_total,
            jnp.sum(up_grad.astype(jnp.float32), axis=0),
            back_total,
        ]
    )
    grads = (grad_qkv_w, grad_out_w, grad_up_w, grad_down_w, vector_grad)
    whole = lax.psum((grads[0], grads[1], grads[2], grads[3], grads[4]), "dp")
    shares = (
        lax.psum_scatter(whole[0], "zero", scatter_dimension=0, tiled=True),
        lax.psum_scatter(whole[1], "zero", scatter_dimension=0, tiled=True),
        lax.psum_scatter(whole[2], "zero", scatter_dimension=0, tiled=True),
        lax.psum_scatter(whole[3], "zero", scatter_dimension=0, tiled=True),
        lax.psum_scatter(whole[4], "zero", scatter_dimension=0, tiled=True),
    )
    qkv_new = adamw(qkv_weight, qkv_first, qkv_second, shares[0], RATE_MATRIX)
    out_new = adamw(out_weight, out_first, out_second, shares[1], RATE_OUTPUT)
    up_new = adamw(up_weight, up_first, up_second, shares[2], RATE_MATRIX)
    down_new = adamw(down_weight, down_first, down_second, shares[3], RATE_MATRIX)
    vec_new = adamw(vectors, vectors_first, vectors_second, shares[4], RATE_VECTOR)
    return (
        activations,
        input_grad,
        qkv_new[0],
        out_new[0],
        up_new[0],
        down_new[0],
        vec_new[0],
        qkv_new[1],
        out_new[1],
        up_new[1],
        down_new[1],
        vec_new[1],
        qkv_new[2],
        out_new[2],
        up_new[2],
        down_new[2],
        vec_new[2],
    )


def solution(mesh):
    placed = (
        P(("dp", "zero"), None),
        P(("dp", "zero"), None),
        P(("dp", "zero"), None),
        P("zero", None),
        P("zero", None),
        P("zero", None),
        P("zero", None),
        P("zero"),
        P("zero", None),
        P("zero", None),
        P("zero", None),
        P("zero", None),
        P("zero"),
        P("zero", None),
        P("zero", None),
        P("zero", None),
        P("zero", None),
        P("zero"),
    )
    return jax.shard_map(
        on_device,
        mesh=mesh,
        in_specs=placed,
        out_specs=(
            P(("dp", "zero"), None),
            P(("dp", "zero"), None),
            P("zero", None),
            P("zero", None),
            P("zero", None),
            P("zero", None),
            P("zero"),
            P("zero", None),
            P("zero", None),
            P("zero", None),
            P("zero", None),
            P("zero"),
            P("zero", None),
            P("zero", None),
            P("zero", None),
            P("zero", None),
            P("zero"),
        ),
        check_vma=False,
    )
```

profile of v0, /device:TPU:0, one launch (start us, length us, event | category | flops | bytes accessed | tf_op | source)
XLA Modules:
  0.0 233.7 jit_solution(7566693944684542090)
XLA Ops:
  7.9 1.3 fusion.76
  10.2 8.5 %all-reduce = bf16[3328]{0:T(1024)(128)(2,1)S(1)} all-reduce(bf16[3328]{0:T(1024)(128)(2,1)S(1)} %dynamic-update-slice), channel_id=1, replica_groups=mesh['dp'=8,'zero'=4] {'zero'}, use_global_device_ids=true, to_apply=%add | all-reduce | flops 3328 | bytes 13312
  18.7 1.1 convert_reduce_fusion.2
  19.8 1.2 fusion.38
  22.0 6.1 %all_gather.16 = bf16[256,768]{1,0:T(8,128)(2,1)S(1)} all-gather(bf16[64,768]{1,0:T(8,128)(2,1)S(1)} %convert_element_type.126), channel_id=1, replica_groups=mesh['dp'=8,'zero'=4] {'zero'}, dimensions={0}, use_global_device_ids=true | all-gather | bytes 491520 | tf_op jit(solution)/shard_map/all_gather | solution.py:176
  28.1 1.4 convolution_add_fusion
  33.5 1.6 fusion.78
  35.1 1.2 fusion
  36.3 2.1 copy-done
  38.4 1.5 fusion.21
  41.1 5.6 %all_gather.17 = bf16[256,256]{1,0:T(8,128)(2,1)S(1)} all-gather(bf16[64,256]{1,0:T(8,128)(2,1)S(1)} %convert_element_type.134), channel_id=1, replica_groups=mesh['dp'=8,'zero'=4] {'zero'}, dimensions={0}, use_global_device_ids=true | all-gather | bytes 163840 | tf_op jit(solution)/shard_map/all_gather | solution.py:177
  47.0 5.5 %multiply_reduce_fusion = (f32[8,512]{1,0:T(8,128)S(1)}, f32[8,512,512]{1,2,0:T(8,128)S(1)}) fusion(f32[8,512,512]{1,2,0:T(8,128)} %copy-done, f32[8,512]{1,0:T(8,128)S(1)} %log_add_fusion, bf16[512,8,32]{0,2,1:T(8,128)(2,1)S(1)} %bitcast.49, bf16[512,8,32]{0,2,1:T(8,128)(2,1)S(1)} %bitcast.60), kind=kOutput, calls=%fused_computation.1 | convolution fusion | flops 140505088 | bytes 17334272 | tf_op jit(solution)/shard_map/while/body/eval_jaxpr/qhd,khd->hqk/dot_general | solution.py:117
  53.0 2.5 %multiply_convert_fusion = bf16[8,512,512]{1,2,0:T(8,128)(2,1)S(1)} fusion(f32[8,512,512]{1,2,0:T(8,128)S(1)} %get-tuple-element.121, f32[8,512,512]{1,2,0:T(8,128)S(1)} %bitcast.46, f32[8,512]{1,0:T(8,128)S(1)} %get-tuple-element.120, f32[8,512]{1,0:T(8,128)S(1)} %log_add_fusion), kind=kLoop, calls=%fused_computation | loop fusion | flops 8388608 | bytes 21004288 | tf_op jit(solution)/shard_map/while/body/eval_jaxpr/convert_element_type | solution.py:120
  56.3 1.3 fusion.13
  57.6 1.4 fusion.18
  60.0 1.5 fusion.44
  61.6 7.3 %all_gather.18 = bf16[256,1024]{1,0:T(8,128)(2,1)S(1)} all-gather(bf16[64,1024]{1,0:T(8,128)(2,1)S(1)} %convert_element_type.136), channel_id=1, replica_groups=mesh['dp'=8,'zero'=4] {'zero'}, dimensions={0}, use_global_device_ids=true | all-gather | bytes 655360 | tf_op jit(solution)/shard_map/all_gather | solution.py:178
  68.9 7.5 %all_gather.19 = bf16[1024,256]{1,0:T(8,128)(2,1)S(1)} all-gather(bf16[256,256]{1,0:T(8,128)(2,1)S(1)} %convert_element_type.138), channel_id=1, replica_groups=mesh['dp'=8,'zero'=4] {'zero'}, dimensions={0}, use_global_device_ids=true | all-gather | bytes 655360 | tf_op jit(solution)/shard_map/all_gather | solution.py:179
  76.4 4.8 %multiply_convert_fusion.1 = (bf16[512,1024]{1,0:T(8,128)(2,1)S(1)}, f32[512,1024]{1,0:T(8,128)S(1)}, f32[512,1024]{1,0:T(8,128)S(1)}) fusion(f32[1024]{0:T(1024)S(1)} %slice.100, bf16[256,1024]{1,0:T(8,128)(2,1)S(1)} %all_gather.18, bf16[512,256]{1,0:T(8,128)(2,1)S(1)} %copy-done.1, f32[256]{0:T(256)S(1)} %get-tuple-element.106, ...), kind=kOutput, calls=%fused_computation.15 | convolution fusion | flops 303824896 | bytes 6039552 | tf_op jit(solution)/shard_map/dot_general | solution.py:204
  81.2 1.2 convert_reduce_fusion
  83.4 1.6 fusion.55
  85.1 1.6 fusion.61
  86.7 1.2 fusion.45
  88.1 2.1 fusion.37
  91.7 23.5 %reduce-scatter.9.cloned.1.call-done = f32[64,1024]{1,0:T(8,128)} async-done(((f32[256,1024]{1,0:T(8,128)}), f32[64,1024]{1,0:T(8,128)}) %reduce-scatter.9.cloned.1.call-update) | async-done | bytes 262160 | tf_op jit(solution)/shard_map/reduce_scatter | solution.py:249
  115.3 27.5 %reduce-scatter.11.cloned.1.call-done = f32[256,256]{1,0:T(8,128)} async-done(((f32[1024,256]{1,0:T(8,128)}), f32[256,256]{1,0:T(8,128)}) %reduce-scatter.11.cloned.1.call-update) | async-done | bytes 262160 | tf_op jit(solution)/shard_map/reduce_scatter | solution.py:250
  143.5 10.1 %all-reduce.1 = f32[3328]{0:T(1024)S(1)} all-reduce(f32[3328]{0:T(1024)S(1)} %constant_dynamic-update-slice_fusion), channel_id=6, replica_groups=mesh['dp'=8,'zero'=4] {'zero'}, use_global_device_ids=true, to_apply=%region_23.24.clone | all-reduce | flops 3328 | bytes 26624
  153.7 21.5 %psum.44 = f32[832]{0:T(1024)S(1)} all-reduce(f32[832]{0:T(1024)S(1)} %dynamic-slice.2), channel_id=1, replica_groups=mesh['dp'=8,'zero'=4] {'dp'}, use_global_device_ids=true, to_apply=%region_22.23 | all-reduce | flops 832 | bytes 6656 | tf_op jit(solution)/shard_map/psum | solution.py:245
  176.1 1.1 fusion.17
  177.3 44.3 %all-reduce.5.cloned.1.call-done = (f32[64,768]{1,0:T(8,128)}, f32[64,256]{1,0:T(8,128)}, f32[64,1024]{1,0:T(8,128)}, f32[256,256]{1,0:T(8,128)}) async-done(((f32[64,768]{1,0:T(8,128)}, f32[64,256]{1,0:T(8,128)}, f32[64,1024]{1,0:T(8,128)}, f32[256,256]{1,0:T(8,128)}), (f32[64,768]{1,0:T(8,128)}, f32[64,256]{1,0:T(8,128)}, f32[64,1024]{1,0:T(8,128)}, f32[256,256]{1,0:T(8,128)})) %all-reduce.5.cloned.1.call-update) | async-done | bytes 786448 | tf_op jit(solution)/shard_map/psum | solution.py:245
  221.6 2.0 multiply_subtract_fusion
  223.6 1.9 multiply_subtract_fusion.1
  (124 shorter events, 13.4 us)
Async XLA Ops:
  7.2 84.5 %reduce-scatter.7.cloned.1.call-start = ((), (), s32[]{:S(2)}) async-start(), calls=%async_computation.5 | async-start | bytes 327680 | tf_op jit(solution)/shard_map/reduce_scatter | solution.py:248
  28.1 1.6 copy-start.27
  35.1 3.3 %copy-start = (f32[8,512,512]{1,2,0:T(8,128)}, f32[8,512,512]{1,2,0:T(8,128)S(1)}, u32[]{:S(2)}) copy-start(f32[8,512,512]{1,2,0:T(8,128)S(1)} %get-tuple-element.118) | copy-start | bytes 25165828
  38.4 2.7 %copy-start.17 = (f32[64,256]{1,0:T(8,128)S(1)}, f32[64,256]{1,0:T(8,128)}, u32[]{:S(2)}) copy-start(f32[64,256]{1,0:T(8,128)} %param.22) | copy-start | bytes 196612
  39.9 12.6 %copy-start.7 = (bf16[8,32,512]{2,1,0:T(8,128)(2,1)}, bf16[8,32,512]{2,1,0:T(8,128)(2,1)S(1)}, u32[]{:S(2)}) copy-start(bf16[8,32,512]{2,1,0:T(8,128)(2,1)S(1)} %fusion.21) | copy-start | bytes 786436
  41.0 50.7 %reduce-scatter.5.cloned.1.call-start = ((), (), s32[]{:S(2)}) async-start(), calls=%async_computation.4 | async-start | bytes 983040 | tf_op jit(solution)/shard_map/reduce_scatter | solution.py:247
  47.0 5.5 %slice-start = ((s8[8388608]{0:T(1024)(128)(4,1)}), s8[4194304]{0:T(1024)(128)(4,1)S(1)}, s32[]{:S(2)}) async-start(s8[8388608]{0:T(1024)(128)(4,1)} %bitcast.45), calls=%async_computation.9 | async-start | bytes 8388608
  47.0 6.0 %slice-start.1 = ((s8[8388608]{0:T(1024)(128)(4,1)}), s8[4194304]{0:T(1024)(128)(4,1)S(1)}, s32[]{:S(2)}) async-start(s8[8388608]{0:T(1024)(128)(4,1)} %bitcast.45), calls=%async_computation.10 | async-start | bytes 8388608
  59.2 2.4 %copy-start.5 = (f32[64,1024]{1,0:T(8,128)S(1)}, f32[64,1024]{1,0:T(8,128)}, u32[]{:S(2)}) copy-start(f32[64,1024]{1,0:T(8,128)} %param.23) | copy-start | bytes 786436
  60.0 8.9 %copy-start.3 = (f32[256,256]{1,0:T(8,128)S(1)}, f32[256,256]{1,0:T(8,128)}, u32[]{:S(2)}) copy-start(f32[256,256]{1,0:T(8,128)} %param.24) | copy-start | bytes 786436
  61.5 53.8 %reduce-scatter.9.cloned.1.call-start = ((), (), s32[]{:S(2)}) async-start(), calls=%async_computation.6 | async-start | bytes 1310720 | tf_op jit(solution)/shard_map/reduce_scatter | solution.py:249
  68.9 12.3 %copy-start.11 = (bf16[256,1024]{1,0:T(8,128)(2,1)}, bf16[256,1024]{1,0:T(8,128)(2,1)S(1)}, u32[]{:S(2)}) copy-start(bf16[256,1024]{1,0:T(8,128)(2,1)S(1)} %all_gather.18) | copy-start | bytes 1572868
  85.0 57.7 %reduce-scatter.11.cloned.1.call-start = ((), (), s32[]{:S(2)}) async-start(), calls=%async_computation.7 | async-start | bytes 1310720 | tf_op jit(solution)/shard_map/reduce_scatter | solution.py:250
  86.7 134.8 %all-reduce.5.cloned.1.call-start = ((), (), s32[]{:S(2)}) async-start(), calls=%async_computation.8 | async-start | bytes 1572864 | tf_op jit(solution)/shard_map/psum | solution.py:245
  87.9 2.4 %copy-start.12 = (f32[512,256]{1,0:T(8,128)S(1)}, f32[512,256]{1,0:T(8,128)}, u32[]{:S(2)}) copy-start(f32[512,256]{1,0:T(8,128)} %fusion.45) | copy-start | bytes 1572868
  90.2 84.9 %copy-start.24 = (f32[832]{0:T(1024)S(1)}, f32[832]{0:T(1024)}, u32[]{:S(2)}) copy-start(f32[832]{0:T(1024)} %param.25) | copy-start | bytes 9988
  90.2 84.9 %copy-start.25 = (f32[832]{0:T(1024)S(1)}, f32[832]{0:T(1024)}, u32[]{:S(2)}) copy-start(f32[832]{0:T(1024)} %param.30) | copy-start | bytes 9988
  90.3 84.9 %copy-start.26 = (f32[832]{0:T(1024)S(1)}, f32[832]{0:T(1024)}, u32[]{:S(2)}) copy-start(f32[832]{0:T(1024)} %param.35) | copy-start | bytes 9988
  90.3 85.5 %copy-start.8 = (bf16[8,32,512]{2,1,0:T(8,128)(2,1)S(1)}, bf16[8,32,512]{2,1,0:T(8,128)(2,1)}, u32[]{:S(2)}) copy-start(bf16[8,32,512]{2,1,0:T(8,128)(2,1)} %copy-done.7) | copy-start | bytes 786436
  142.7 78.8 %copy-start.4 = (f32[256,256]{1,0:T(8,128)S(1)}, f32[256,256]{1,0:T(8,128)}, u32[]{:S(2)}) copy-start(f32[256,256]{1,0:T(8,128)} %param.24) | copy-start | bytes 786436
  142.7 78.8 %copy-start.13 = (f32[256,256]{1,0:T(8,128)S(1)}, f32[256,256]{1,0:T(8,128)}, u32[]{:S(2)}) copy-start(f32[256,256]{1,0:T(8,128)} %param.29) | copy-start | bytes 786436
  142.7 78.8 %copy-start.14 = (f32[256,256]{1,0:T(8,128)S(1)}, f32[256,256]{1,0:T(8,128)}, u32[]{:S(2)}) copy-start(f32[256,256]{1,0:T(8,128)} %param.34) | copy-start | bytes 786436
  176.1 47.5 %copy-start.6 = (f32[64,1024]{1,0:T(8,128)S(1)}, f32[64,1024]{1,0:T(8,128)}, u32[]{:S(2)}) copy-start(f32[64,1024]{1,0:T(8,128)} %param.23) | copy-start | bytes 786436
  176.1 47.5 %copy-start.15 = (f32[64,1024]{1,0:T(8,128)S(1)}, f32[64,1024]{1,0:T(8,128)}, u32[]{:S(2)}) copy-start(f32[64,1024]{1,0:T(8,128)} %param.28) | copy-start | bytes 786436
  176.1 47.5 %copy-start.16 = (f32[64,1024]{1,0:T(8,128)S(1)}, f32[64,1024]{1,0:T(8,128)}, u32[]{:S(2)}) copy-start(f32[64,1024]{1,0:T(8,128)} %param.33) | copy-start | bytes 786436
  177.2 48.3 %copy-start.10 = (f32[64,768]{1,0:T(8,128)S(1)}, f32[64,768]{1,0:T(8,128)}, u32[]{:S(2)}) copy-start(f32[64,768]{1,0:T(8,128)} %param.21) | copy-start | bytes 589828
  177.2 48.3 %copy-start.18 = (f32[64,768]{1,0:T(8,128)S(1)}, f32[64,768]{1,0:T(8,128)}, u32[]{:S(2)}) copy-start(f32[64,768]{1,0:T(8,128)} %param.26) | copy-start | bytes 589828
  177.2 48.3 %copy-start.19 = (f32[64,768]{1,0:T(8,128)S(1)}, f32[64,768]{1,0:T(8,128)}, u32[]{:S(2)}) copy-start(f32[64,768]{1,0:T(8,128)} %param.31) | copy-start | bytes 589828
  221.5 4.0 %copy-start.20 = (f32[64,768]{1,0:T(8,128)S(1)}, f32[64,768]{1,0:T(8,128)}, u32[]{:S(2)}) copy-start(f32[64,768]{1,0:T(8,128)} %get-tuple-element.73) | copy-start | bytes 589828
  221.5 4.9 %copy-start.21 = (f32[64,256]{1,0:T(8,128)S(1)}, f32[64,256]{1,0:T(8,128)}, u32[]{:S(2)}) copy-start(f32[64,256]{1,0:T(8,128)} %param.27) | copy-start | bytes 196612
  221.5 4.9 %copy-start.22 = (f32[64,256]{1,0:T(8,128)S(1)}, f32[64,256]{1,0:T(8,128)}, u32[]{:S(2)}) copy-start(f32[64,256]{1,0:T(8,128)} %param.32) | copy-start | bytes 196612
  221.5 4.9 %copy-start.23 = (f32[64,256]{1,0:T(8,128)S(1)}, f32[64,256]{1,0:T(8,128)}, u32[]{:S(2)}) copy-start(f32[64,256]{1,0:T(8,128)} %get-tuple-element.74) | copy-start | bytes 196612
  (3 other events, 3.5 us)
Sparse Core Ops, SparseCore 0:
  41.1 20.6 reduce-scatter.6
  64.5 23.2 reduce-scatter.4
  90.3 24.8 reduce-scatter.8
  117.8 24.8 reduce-scatter.10
  146.3 75.1 all-reduce.4
where the time goes:
time: 234 us
  waiting for transfers between devices  95.4 us (41%)
  blocking collectives  66.6 us (28%)
  matrix products  30.3 us (13%)
  between operations  17.1 us (7%)
  other arithmetic  16.8 us (7%)
  local copies, waits for them, and re-layouts  7.3 us (3%)
    psum x1, waiting for transfers between devices, on_device(): whole = lax.psum((grads[0], grads[1], grads[2], grads[3], grads[4]), 'dp')  44.3 us
    reduce_scatter x1, waiting for transfers between devices, on_device(): lax.psum_scatter(whole[3], 'zero', scatter_dimension=0, tiled=True)  27.5 us
    reduce_scatter x1, waiting for transfers between devices, on_device(): lax.psum_scatter(whole[2], 'zero', scatter_dimension=0, tiled=True)  23.5 us
    psum x1, blocking collectives, on_device(): whole = lax.psum((grads[0], grads[1], grads[2], grads[3], grads[4]), 'dp')  21.5 us
    unnamed x2, blocking collectives  18.6 us
    all_gather x1, blocking collectives, on_device(): lax.all_gather(down_weight.astype(jnp.bfloat16), 'zero', axis=0, tiled=True)  7.51 us
    all_gather x1, blocking collectives, on_device(): lax.all_gather(up_weight.astype(jnp.bfloat16), 'zero', axis=0, tiled=True)  7.29 us
    sub x5, other arithmetic, adamw(): return (master - rate * (direction + DECAY * master), momentum, variance)  6.17 us
  transfers between devices with their start and end apart: 5, of which 3 were waited for; matrix products, arithmetic and copies ran while one was open for 13% of the time, Pallas kernels for 0%

commit v1 on v0

v1 whole, which is shorter than its diff:
```python
import functools
import math

import jax
import jax.numpy as jnp
from jax import lax
from jax.experimental import pallas as pl
from jax.experimental.pallas import tpu as pltpu
from jax.sharding import PartitionSpec as P

HEADS = 8
HEAD_DIM = 32
ROT = 8
STEP = 5


NORM_EPS = 1e-05
BETA_ONE = 0.9
BETA_TWO = 0.95
ADAM_EPS = 1e-08
DECAY = 0.01
RATE_MATRIX = 0.06
RATE_OUTPUT = 0.3
RATE_VECTOR = 0.5
NEGATIVE = -1e30
MESH = pl.DeviceIdType.MESH
F32 = jnp.float32
BF16 = jnp.bfloat16
VROWS = 32
W = 256


def adamw(master, first, second, grad, rate):
    momentum = BETA_ONE * first + (1.0 - BETA_ONE) * grad
    variance = BETA_TWO * second + (1.0 - BETA_TWO) * grad * grad
    direction = (
        momentum / (1.0 - BETA_ONE**STEP) / (jnp.sqrt(variance / (1.0 - BETA_TWO**STEP)) + ADAM_EPS)
    )
    return (master - rate * (direction + DECAY * master), momentum, variance)


def nn(a, b):
    return lax.dot_general(a, b, (((1,), (0,)), ((), ())), preferred_element_type=F32)


def nt(a, b):
    return lax.dot_general(a, b, (((1,), (1,)), ((), ())), preferred_element_type=F32)


def tn(a, b):
    return lax.dot_general(a, b, (((0,), (0,)), ((), ())), preferred_element_type=F32)


def remote(src, dst, send, recv, device):
    return pltpu.make_async_remote_copy(
        src_ref=src, dst_ref=dst, send_sem=send, recv_sem=recv, device_id=device, device_id_type=MESH
    )


class Reduction:
    def __init__(self, place, full, core_in, y_out, y_in, share, share_low, pieces, total, sems):
        self.place = place
        self.full, self.core_in, self.y_out, self.y_in = full, core_in, y_out, y_in
        self.share, self.share_low, self.pieces, self.total = share, share_low, pieces, total
        self.zs, self.zr, self.ds, self.dr, self.gs, self.gr = sems
        self.piece = pieces.shape[1]
        self.rows = full.shape[2]

    def core_copy(self, slot):
        p = self.place
        y = p.y if slot else 1 - p.y
        return remote(
            self.full.at[1 - p.c, y], self.core_in.at[y], self.zs.at[slot], self.zr.at[slot], {"zero": p.core}
        )

    def y_copy(self):
        return remote(self.y_out, self.y_in, self.zs.at[2], self.zr.at[2], {"zero": self.place.other})

    def rows_of(self, index):
        return pl.ds(pl.multiple_of(index * self.piece, self.piece), self.piece)

    def scatter_copy(self, k):
        p = self.place
        peer = lax.rem(p.dp + k, p.n)
        return remote(
            self.share_low.at[self.rows_of(peer)], self.pieces.at[k], self.ds.at[k], self.dr.at[k], {"dp": peer}
        )

    def gather_copy(self, k):
        p = self.place
        peer = lax.rem(p.dp + k, p.n)
        mine = self.total.at[self.rows_of(p.dp)]
        return remote(mine, mine, self.gs.at[k], self.gr.at[k], {"dp": peer})

    def gather_arrival(self, k):
        p = self.place
        peer = lax.rem(p.dp + p.n - k, p.n)
        theirs = self.total.at[self.rows_of(peer)]
        return remote(theirs, theirs, self.gs.at[k], self.gr.at[k], {"dp": peer})

    def loop(self, action):
        def body(k, carry):
            action(k)
            return carry

        lax.fori_loop(1, self.place.n, body, 0)

    def stage_core(self):
        self.core_copy(0).start()
        self.core_copy(1).start()

    def stage_y(self):
        p = self.place
        self.core_copy(0).wait_recv()
        self.y_out[...] = (self.full[p.c, 1 - p.y] + self.core_in[1 - p.y]).astype(BF16)
        self.y_copy().start()

    def stage_scatter(self):
        p = self.place
        self.core_copy(1).wait_recv()
        self.y_copy().wait_recv()
        summed = self.full[p.c, p.y] + self.core_in[p.y] + self.y_in[...].astype(F32)
        self.share[pl.ds(0, self.rows)] = summed
        self.share_low[pl.ds(0, self.rows)] = summed.astype(BF16)
        spare = self.share.shape[0] - self.rows
        if spare:
            self.share[pl.ds(self.rows, spare)] = jnp.zeros((spare, W), F32)
            self.share_low[pl.ds(self.rows, spare)] = jnp.zeros((spare, W), BF16)
        self.loop(lambda k: self.scatter_copy(k).start())

    def stage_gather(self):
        p = self.place
        self.loop(lambda k: self.scatter_copy(k).wait_recv())
        summed = self.share[self.rows_of(p.dp)]
        if p.n <= 16:
            for k in range(1, p.n):
                summed = summed + self.pieces[k].astype(F32)
        else:
            summed = lax.fori_loop(1, p.n, lambda k, s: s + self.pieces[k].astype(F32), summed)
        self.total[self.rows_of(p.dp)] = summed.astype(self.total.dtype)
        self.loop(lambda k: self.gather_copy(k).start())

    def stage_end(self):
        self.loop(lambda k: self.gather_arrival(k).wait_recv())

    def drain(self):
        self.core_copy(0).wait_send()
        self.core_copy(1).wait_send()
        self.y_copy().wait_send()
        self.loop(lambda k: self.scatter_copy(k).wait_send())
        self.loop(lambda k: self.gather_copy(k).wait_send())


class Place:
    def __init__(self, n):
        self.n = n
        self.dp = lax.axis_index("dp")
        self.z = lax.axis_index("zero")
        self.c = lax.rem(self.z, 2)
        self.y = self.z // 2
        self.core = 2 * self.y + 1 - self.c
        self.other = 2 * (1 - self.y) + self.c
        self.far = 2 * (1 - self.y) + 1 - self.c


def layer_kernel(
    n,
    lengths, tokens, cotangent, qkv_s, out_s, up_s, down_s, vec_s,
    act_o, ig_o, ga_o, gc_o, vec_o,
    qkv_w, out_w, up_w, down_w, vec_in, vec_g, vec_z, vec_t, vec_d,
    gat_s, gat_r, vs, vr, vds, vdr,
    bias_m, q_t, k_t, v_t, do_t, o_t, dlin_t, base, dh2_s,
    a_full, a_core, a_yo, a_yi, a_sh, a_shl, a_pc, a_tot, a_zs, a_zr, a_ds, a_dr, a_gs, a_gr,
    c_full, c_core, c_yo, c_yi, c_sh, c_shl, c_pc, c_tot, c_zs, c_zr, c_ds, c_dr, c_gs, c_gr,
):
    p = Place(n)
    count = tokens.shape[0]
    peers_zero = (p.core, p.other, p.far)
    group_a = Reduction(p, a_full, a_core, a_yo, a_yi, a_sh, a_shl, a_pc, a_tot, (a_zs, a_zr, a_ds, a_dr, a_gs, a_gr))
    group_c = Reduction(p, c_full, c_core, c_yo, c_yi, c_sh, c_shl, c_pc, c_tot, (c_zs, c_zr, c_ds, c_dr, c_gs, c_gr))

    barrier = pltpu.get_barrier_semaphore()
    for peer in peers_zero:
        pl.semaphore_signal(barrier, inc=1, device_id={"zero": peer}, device_id_type=MESH)

    def greet(k, carry):
        peer = lax.rem(p.dp + k, n)
        pl.semaphore_signal(barrier, inc=1, device_id={"dp": peer}, device_id_type=MESH)
        return carry

    lax.fori_loop(1, n, greet, 0)

    weights = (qkv_w, out_w, up_w, down_w)
    for buffer, shard in zip(weights, (qkv_s, out_s, up_s, down_s)):
        buffer[p.z] = shard[...].astype(BF16)
    pl.semaphore_wait(barrier, 3 + n - 1)

    def vec_copy(i, src, dst):
        return remote(src, dst.at[i], vs.at[i], vr.at[i], {"zero": peers_zero[i]})

    def weight_copy(w, way):
        buffer = weights[w]
        shard = p.other if way == 2 else p.z
        device = p.other if way == 1 else p.core
        return remote(buffer.at[shard], buffer.at[shard], gat_s.at[w, way], gat_r.at[w, way], {"zero": device})

    def weight_arrival(w, way):
        buffer = weights[w]
        shard = (p.core, p.other, p.far)[way]
        device = p.other if way == 1 else p.core
        return remote(buffer.at[shard], buffer.at[shard], gat_s.at[w, way], gat_r.at[w, way], {"zero": device})

    for i in range(3):
        vec_copy(i, vec_s, vec_in).start()
    for w in range(4):
        weight_copy(w, 1).start()
        weight_copy(w, 0).start()

    first = lengths[0, 0]
    total = lengths[0, 0] + lengths[0, 1]
    index = lax.broadcasted_iota(jnp.int32, (1, count), 1)
    start = jnp.where(index >= total, total, jnp.where(index >= first, first, 0))
    live = jnp.where(index < total, 1.0, 0.0).astype(F32)
    key_index = lax.broadcasted_iota(jnp.int32, (count, count), 0)
    query_index = lax.broadcasted_iota(jnp.int32, (count, count), 1)
    bias_m[...] = jnp.where((key_index <= query_index) & (key_index >= start), 0.0, NEGATIVE).astype(F32)
    half = ROT // 2
    row = lax.broadcasted_iota(jnp.int32, (ROT, count), 0)
    turn = lax.rem(row, half)
    freq = jnp.where(turn == 0, 1.0, jnp.where(turn == 1, 0.1, jnp.where(turn == 2, 0.01, 0.001))).astype(F32)
    angle = (index - start).astype(F32) * freq
    cosine = jnp.cos(angle)
    sine = jnp.sin(angle) * jnp.where(row < half, -1.0, 1.0).astype(F32)

    def rotate(lines, signed):
        top = lines[:ROT]
        swapped = jnp.concatenate([top[half:], top[:half]], axis=0)
        return jnp.concatenate([top * cosine + swapped * signed, lines[ROT:]], axis=0)

    x = tokens[...].astype(F32).T
    g = (cotangent[...].astype(F32).T * live).astype(BF16)
    centered = x - jnp.mean(x, axis=0, keepdims=True)
    rstd = lax.rsqrt(jnp.mean(centered * centered, axis=0, keepdims=True) + NORM_EPS)
    plain = centered * rstd

    for i in range(3):
        vec_copy(i, vec_s, vec_in).wait_recv()
    vec = (vec_s[...] + vec_in[0] + vec_in[1] + vec_in[2]).astype(BF16).astype(F32).T

    def column(begin, length):
        parts = [vec[:, i : i + 1] for i in range(begin // 128, (begin + length) // 128)]
        return jnp.concatenate(parts, axis=0)

    gain_one, bias_one, gain_two, bias_two = (column(W * i, W) for i in range(4))
    h1 = (plain * gain_one + bias_one).astype(BF16)
    h2 = (plain * gain_two + bias_two).astype(BF16)

    def finish_weight(w):
        weight_arrival(w, 0).wait_recv()
        weight_arrival(w, 2).wait_recv()

    weight_arrival(0, 1).wait_recv()
    weight_copy(0, 2).start()
    weight_arrival(1, 1).wait_recv()
    weight_copy(1, 2).start()
    finish_weight(0)

    scale = HEAD_DIM**-0.5
    for part, target in enumerate((q_t, k_t, v_t)):
        block = qkv_w[:, :, W * part : W * part + W].reshape(W, W)
        lines = tn(block, h1) + column(4 * W + W * part, W)
        for h in range(HEADS):
            piece = lines[HEAD_DIM * h : HEAD_DIM * h + HEAD_DIM]
            if part < 2:
                piece = rotate(piece, sine)
            target[HEAD_DIM * h : HEAD_DIM * h + HEAD_DIM] = piece.astype(BF16)
    finish_weight(1)
    do_t[...] = nn(out_w[...].reshape(W, W), g).astype(BF16)

    weight_arrival(2, 1).wait_recv()
    weight_copy(2, 2).start()

    fold = scale * math.log2(math.e)
    block = count // 2

    def head(h, carry):
        at = pl.ds(pl.multiple_of(h * HEAD_DIM, HEAD_DIM), HEAD_DIM)
        q, k, v, do = q_t[at], k_t[at], v_t[at], do_t[at]
        outs, dqs, dks, dvs = [], [], [], []
        for j in range(2):
            keys = block * (j + 1)
            cut = slice(block * j, block * (j + 1))
            kk, vv, qj, dj = k[:, :keys], v[:, :keys], q[:, cut], do[:, cut]
            scores = tn(kk, qj) * fold + bias_m[:keys, cut]
            raised = jnp.exp2(scores - jnp.max(scores, axis=0, keepdims=True))
            chances = raised * (1.0 / jnp.sum(raised, axis=0, keepdims=True))
            low = chances.astype(BF16)
            outs.append(nn(vv, low))
            inner = tn(vv, dj)
            slope = (chances * (inner - jnp.sum(inner * chances, axis=0, keepdims=True))).astype(BF16)
            dqs.append(nn(kk, slope))
            dks.append(nt(qj, slope))
            dvs.append(nt(dj, low))
        o_t[at] = jnp.concatenate(outs, axis=1).astype(BF16)
        dq = jnp.concatenate(dqs, axis=1) * scale
        dk = jnp.concatenate([dks[0] + dks[1][:, :block], dks[1][:, block:]], axis=1) * scale
        dv = jnp.concatenate([dvs[0] + dvs[1][:, :block], dvs[1][:, block:]], axis=1)
        dlin_t[0, at] = rotate(dq, -sine).astype(BF16)
        dlin_t[1, at] = rotate(dk, -sine).astype(BF16)
        dlin_t[2, at] = dv.astype(BF16)
        return carry

    lax.fori_loop(0, 2, head, 0)
    weight_arrival(3, 1).wait_recv()
    weight_copy(3, 2).start()
    finish_weight(2)
    finish_weight(3)

    ones = jnp.ones((8, count), BF16)

    def put_sum(at, values):
        sums = nt(ones, values)
        for i in range(values.shape[0] // 128):
            vec_g[at // 128 + i : at // 128 + i + 1] = sums[0:1, 128 * i : 128 * i + 128]

    def put_sum_wide(at, values):
        high = values.astype(BF16)
        rest = (values - high.astype(F32)).astype(BF16)
        sums = nt(ones, high) + nt(ones, rest)
        for i in range(values.shape[0] // 128):
            vec_g[at // 128 + i : at // 128 + i + 1] = sums[0:1, 128 * i : 128 * i + 128]

    shard_rows = W // 4
    mlp = jnp.zeros((W, count), F32)
    dh2 = jnp.zeros((W, count), F32)
    for j in range(4):
        w_up = up_w[:, :, W * j : W * j + W].reshape(W, W)
        w_down = down_w[j]
        up = tn(w_up, h2) + column(8 * W + W * j, W)
        phi_sum = 0.5 + 0.5 * lax.erf(up * (0.5**0.5))
        z = (up * phi_sum).astype(BF16)
        bell = jnp.exp2(up * up * (-0.5 * math.log2(math.e))) * ((2.0 * math.pi) ** -0.5)
        du = (nn(w_down, g) * (phi_sum + up * bell)).astype(BF16)
        mlp = mlp + tn(w_down, z)
        dh2 = dh2 + nn(w_up, du)
        a_full[j % 2, j // 2, pl.ds(0, W)] = nt(z, g)
        g_up = nt(h2, du)
        for s in range(4):
            a_full[s % 2, s // 2, pl.ds(W + shard_rows * j, shard_rows)] = g_up[shard_rows * s : shard_rows * (s + 1)]
        put_sum(8 * W + W * j, du)
    group_a.stage_core()
    base[...] = x + mlp + column(12 * W, W)
    dh2_s[...] = dh2

    lax.fori_loop(2, 4, head, 0)
    group_a.stage_y()
    lax.fori_loop(4, 6, head, 0)
    group_a.stage_scatter()
    lax.fori_loop(6, 8, head, 0)

    for j in range(3):
        dlin = dlin_t[j]
        g_qkv = nt(h1, dlin)
        for s in range(4):
            c_full[s % 2, s // 2, pl.ds(shard_rows * j, shard_rows)] = g_qkv[shard_rows * s : shard_rows * (s + 1)]
        put_sum(4 * W + W * j, dlin)
    g_out = nt(o_t[...], g)
    for s in range(4):
        c_full[s % 2, s // 2, pl.ds(3 * shard_rows, shard_rows)] = g_out[shard_rows * s : shard_rows * (s + 1)]
    group_c.stage_core()
    group_a.stage_gather()

    dh1 = jnp.zeros((W, count), F32)
    for j in range(3):
        dh1 = dh1 + nn(qkv_w[:, :, W * j : W * j + W].reshape(W, W), dlin_t[j])
    group_c.stage_y()
    dh2 = dh2_s[...]
    put_sum_wide(0, dh1 * plain)
    put_sum_wide(W, dh1)
    put_sum_wide(2 * W, dh2 * plain)
    put_sum_wide(3 * W, dh2)
    put_sum(7 * W, g)
    put_sum(12 * W, g)
    vec_g[13 * W // 128 : VROWS] = jnp.zeros((VROWS - 13 * W // 128, 128), F32)

    def vec_zero(i):
        return remote(vec_g, vec_z.at[i], vs.at[3 + i], vr.at[3 + i], {"zero": peers_zero[i]})

    for i in range(3):
        vec_zero(i).start()
    group_c.stage_scatter()
    dn = dh1 * gain_one + dh2 * gain_two
    term = (
        dn - jnp.mean(dn, axis=0, keepdims=True) - plain * jnp.mean(dn * plain, axis=0, keepdims=True)
    ) * rstd
    for i in range(3):
        vec_zero(i).wait_recv()
    vec_t[...] = vec_g[...] + vec_z[0] + vec_z[1] + vec_z[2]

    def vec_dp(k):
        peer = lax.rem(p.dp + k, n)
        return remote(vec_t, vec_d.at[k], vds.at[k], vdr.at[k], {"dp": peer})

    group_c.loop(lambda k: vec_dp(k).start())
    ig_o[...] = (g.astype(F32) + term).T.astype(BF16)
    attn = tn(out_w[...].reshape(W, W), o_t[...]) + column(7 * W, W)
    act_o[...] = ((base[...] + attn) * live).T.astype(BF16)

    group_c.stage_gather()
    group_a.stage_end()
    ga_o[...] = a_tot[...].astype(F32)
    group_c.loop(lambda k: vec_dp(k).wait_recv())
    vec_o[...] = lax.fori_loop(1, n, lambda k, s: s + vec_d[k], vec_t[...])
    for w in range(4):
        for way in range(3):
            weight_copy(w, way).wait_send()
    for i in range(3):
        vec_copy(i, vec_s, vec_in).wait_send()
        vec_zero(i).wait_send()
    group_c.loop(lambda k: vec_dp(k).wait_send())
    group_a.drain()
    group_c.stage_end()
    gc_o[...] = c_tot[...].astype(F32)
    group_c.drain()


def piece_rows(rows, n):
    return -(-rows // (16 * n)) * 16


def reduction_scratch(rows, n, kind):
    piece = piece_rows(rows, n)
    dma = pltpu.SemaphoreType.DMA
    return [
        pltpu.VMEM((2, 2, rows, W), F32),
        pltpu.VMEM((2, rows, W), F32),
        pltpu.VMEM((rows, W), BF16),
        pltpu.VMEM((rows, W), BF16),
        pltpu.VMEM((n * piece, W), F32),
        pltpu.VMEM((n * piece, W), BF16),
        pltpu.VMEM((n, piece, W), BF16),
        pltpu.VMEM((n * piece, W), kind),
        dma((3,)), dma((3,)), dma((n,)), dma((n,)), dma((n,)), dma((n,)),
    ]


def layer(n, lengths, tokens, cotangent, qkv, out, up, down, vec):
    count = tokens.shape[0]
    dma = pltpu.SemaphoreType.DMA
    a_rows = n * piece_rows(512, n)
    c_rows = n * piece_rows(256, n)
    vmem = pl.BlockSpec(memory_space=pltpu.VMEM)
    return pl.pallas_call(
        functools.partial(layer_kernel, n),
        out_shape=(
            jax.ShapeDtypeStruct(tokens.shape, BF16),
            jax.ShapeDtypeStruct(tokens.shape, BF16),
            jax.ShapeDtypeStruct((a_rows, W), F32),
            jax.ShapeDtypeStruct((c_rows, W), F32),
            jax.ShapeDtypeStruct((VROWS, 128), F32),
        ),
        in_specs=[pl.BlockSpec(memory_space=pltpu.SMEM)] + [vmem] * 7,
        out_specs=[vmem] * 5,
        scratch_shapes=[
            pltpu.VMEM((4, 64, 3 * W), BF16),
            pltpu.VMEM((4, 64, W), BF16),
            pltpu.VMEM((4, 64, 4 * W), BF16),
            pltpu.VMEM((4, W, W), BF16),
            pltpu.VMEM((3, VROWS, 128), F32),
            pltpu.VMEM((VROWS, 128), F32),
            pltpu.VMEM((3, VROWS, 128), F32),
            pltpu.VMEM((VROWS, 128), F32),
            pltpu.VMEM((n, VROWS, 128), F32),
            dma((4, 3)), dma((4, 3)), dma((6,)), dma((6,)), dma((n,)), dma((n,)),
            pltpu.VMEM((count, count), F32),
            pltpu.VMEM((W, count), BF16),
            pltpu.VMEM((W, count), BF16),
            pltpu.VMEM((W, count), BF16),
            pltpu.VMEM((W, count), BF16),
            pltpu.VMEM((W, count), BF16),
            pltpu.VMEM((3, W, count), BF16),
            pltpu.VMEM((W, count), F32),
            pltpu.VMEM((W, count), F32),
        ]
        + reduction_scratch(512, n, F32)
        + reduction_scratch(256, n, F32),
        compiler_params=pltpu.CompilerParams(
            collective_id=0, has_side_effects=True, vmem_limit_bytes=56 * 1024 * 1024
        ),
        name="layer",
    )(lengths, tokens, cotangent, qkv, out, up, down, vec)


def on_device(
    n,
    tokens,
    cotangent,
    lengths,
    qkv_weight,
    out_weight,
    up_weight,
    down_weight,
    vectors,
    qkv_first,
    out_first,
    up_first,
    down_first,
    vectors_first,
    qkv_second,
    out_second,
    up_second,
    down_second,
    vectors_second,
):
    share = vectors.shape[0]
    begin = lax.axis_index("zero") * share
    vec = lax.dynamic_update_slice(jnp.zeros((VROWS * 128,), F32), vectors, (begin,)).reshape(VROWS, 128)
    activations, input_grad, sum_a, sum_c, sum_vec = layer(
        n, lengths, tokens, cotangent, qkv_weight, out_weight, up_weight, down_weight, vec
    )
    down_sum = sum_a[:W]
    up_sum = sum_a[W : 2 * W].reshape(4, W // 4, W).transpose(1, 0, 2).reshape(W // 4, 4 * W)
    qkv_sum = sum_c[: 3 * W // 4].reshape(3, W // 4, W).transpose(1, 0, 2).reshape(W // 4, 3 * W)
    out_sum = sum_c[3 * W // 4 : W]
    vec_sum = lax.dynamic_slice(sum_vec.reshape(-1), (begin,), (share,))
    qkv_new = adamw(qkv_weight, qkv_first, qkv_second, qkv_sum, RATE_MATRIX)
    out_new = adamw(out_weight, out_first, out_second, out_sum, RATE_OUTPUT)
    up_new = adamw(up_weight, up_first, up_second, up_sum, RATE_MATRIX)
    down_new = adamw(down_weight, down_first, down_second, down_sum, RATE_MATRIX)
    vec_new = adamw(vectors, vectors_first, vectors_second, vec_sum, RATE_VECTOR)
    news = (qkv_new, out_new, up_new, down_new, vec_new)
    return (activations, input_grad) + tuple(new[i] for i in range(3) for new in news)


def solution(mesh):
    tokens = P(("dp", "zero"), None)
    params = (P("zero", None),) * 4 + (P("zero"),)
    return jax.shard_map(
        functools.partial(on_device, mesh.shape["dp"]),
        mesh=mesh,
        in_specs=(tokens,) * 3 + params * 3,
        out_specs=(tokens,) * 2 + params * 3,
        check_vma=False,
    )
```

time: 234 us -> 82.5 us (0.35)
  waiting for transfers between devices: 95.4 us -> 0 us
  Pallas kernels: 0 us -> 67.8 us
  blocking collectives: 66.6 us -> 0 us
  matrix products: 30.3 us -> 0 us
  between operations: 17.1 us -> 0.79 us
  other arithmetic: 16.8 us -> 5.81 us
    pallas_call x0 -> x1, Pallas kernels: none -> 67.8 us  [layer(): pl.pallas_call(functools.partial(layer_kernel, n), out_shape=(jax.ShapeDt...]
    reduce_scatter x4 -> x0, waiting for transfers between devices: 51 us -> none  [the longest x1 27.5 us: on_device(): lax.psum_scatter(whole[3], 'zero', scatter_dimension=0, tiled=True)]
    psum x1 -> x0, waiting for transfers between devices: 44.3 us -> none  [on_device(): whole = lax.psum((grads[0], grads[1], grads[2], grads[3], grads[4]), 'dp')]
    dot_general x18 -> x0, matrix products: 30.3 us -> none  [the longest x1 5.5 us: one_block(): jnp.einsum('qhd,khd->hqk', row_grad, value_heads, preferred_element_type=...]
    all_gather x4 -> x0, blocking collectives: 26.6 us -> none  [the longest x1 7.51 us: on_device(): lax.all_gather(down_weight.astype(jnp.bfloat16), 'zero', axis=0, tiled=True)]
    psum x1 -> x0, blocking collectives: 21.5 us -> none  [on_device(): whole = lax.psum((grads[0], grads[1], grads[2], grads[3], grads[4]), 'dp')]
    unnamed x2 -> x0, blocking collectives: 18.6 us -> none
    reduce_sum x6 -> x0, other arithmetic: 4.92 us -> none  [the longest x2 1.47 us: normalize(): centered = rows - jnp.mean(rows, axis=1, keepdims=True)]
  transfers between devices with their start and end apart: 5 -> 0, of which waited for: 3 -> 0; matrix products, arithmetic and copies ran while one was open for 13% -> 0% of each run, Pallas kernels for 0% -> 0%
where the time goes in v1:
time: 82.5 us; the launch traced here: 82.1 us
  Pallas kernels  67.8 us (82%)
  local copies, waits for them, and re-layouts  7.62 us (9%)
  other arithmetic  5.81 us (7%)
    pallas_call x1, Pallas kernels, layer(): pl.pallas_call(functools.partial(layer_kernel, n), out_shape=(jax.ShapeDt...  67.8 us
    unnamed x41, local copies, waits for them, and re-layouts  6.32 us
    sub x5, other arithmetic, adamw(): return (master - rate * (direction + DECAY * master), momentum, variance)  5.81 us

profile of v1, /device:TPU:0, one launch (start us, length us, event | category | flops | bytes accessed | tf_op | source)
XLA Modules:
  0.0 82.1 jit_solution(15672848985989210318)
XLA Ops:
  0.7 0.7 copy-done.16
  1.3 0.2 dynamic_update_slice.3
  1.5 0.6 copy-done.13
  2.1 67.8 %layer.1 = (bf16[512,256]{1,0:T(8,128)(2,1)}, bf16[512,256]{1,0:T(8,128)(2,1)}, f32[512,256]{1,0:T(8,128)}, f32[256,256]{1,0:T(8,128)}, f32[32,128]{1,0:T(8,128)}) custom-call(s32[1,2]{1,0:T(1,128)} %lengths.1, bf16[512,256]{1,0:T(8,128)(2,1)} %tokens.1, bf16[512,256]{1,0:T(8,128)(2,1)} %cotangent.1, f32[64,768]{1,0:T(8,128)} %qkv_s.1, f32[64,256]{1,0:T(8,128)} %out_s.1, ...), custom_call_target="tpu_custom_call" | custom-call | tf_op jit(solution)/shard_map/layer/pallas_call | solution.py:453
  70.0 0.0 copy-start.18
  70.0 0.0 copy-start.17
  70.0 0.7 copy-done.18
  70.7 0.0 copy-done.17
  70.7 1.4 %multiply_subtract_fusion.4 = (f32[832]{0:T(1024)}, f32[832]{0:T(1024)}, f32[832]{0:T(1024)}) fusion(f32[832]{0:T(1024)S(1)} %copy-done.16, f32[4096]{0:T(1024)} %bitcast.17, s32[]{:T(128)S(6)} %select_n.4, f32[832]{0:T(1024)S(1)} %copy-done.17, f32[832]{0:T(1024)S(1)} %copy-done.18), kind=kLoop, calls=%fused_computation.18 | loop fusion | flops 12480 | bytes 23300 | tf_op jit(solution)/shard_map/sub | solution.py:39
  72.1 1.0 %slice.12 = f32[192,256]{1,0:T(8,128)S(1)} slice(f32[256,256]{1,0:T(8,128)} %get-tuple-element.24), slice={[0:192], [0:256]} | slice | bytes 393216 | tf_op jit(solution)/shard_map/slice | solution.py:523
  73.0 0.0 copy-done.8
  73.1 0.0 copy-done.14
  73.1 0.0 copy-done.15
  73.1 1.5 %multiply_subtract_fusion.3 = (f32[64,256]{1,0:T(8,128)}, f32[64,256]{1,0:T(8,128)}, f32[64,256]{1,0:T(8,128)}) fusion(f32[64,256]{1,0:T(8,128)S(1)} %copy-done.8, f32[256,256]{1,0:T(8,128)} %get-tuple-element.24, f32[64,256]{1,0:T(8,128)S(1)} %copy-done.14, f32[64,256]{1,0:T(8,128)S(1)} %copy-done.15), kind=kLoop, calls=%fused_computation.14 | loop fusion | flops 245760 | bytes 458752 | tf_op jit(solution)/shard_map/sub | solution.py:39
  74.6 0.1 copy.37
  74.8 0.0 copy-start.2
  74.8 0.0 copy-start.11
  74.8 0.7 copy-done.12
  75.5 0.2 copy-done.2
  75.7 0.1 copy-done.11
  75.8 0.9 %multiply_subtract_fusion.2 = (f32[64,768]{1,0:T(8,128)}, f32[64,768]{1,0:T(8,128)}, f32[64,768]{1,0:T(8,128)}) fusion(f32[64,768]{1,0:T(8,128)S(1)} %copy-done.2, f32[64,768]{1,0:T(8,128)S(1)} %bitcast.15, f32[64,768]{1,0:T(8,128)S(1)} %copy-done.11, f32[64,768]{1,0:T(8,128)S(1)} %copy-done.12), kind=kLoop, calls=%fused_computation.10 | loop fusion | flops 737280 | bytes 1376256 | tf_op jit(solution)/shard_map/sub | solution.py:39
  76.7 0.1 copy-done
  76.8 0.4 copy-done.3
  77.1 0.1 copy-done.4
  77.2 0.1 copy-done.5
  77.3 1.0 %multiply_subtract_fusion = (f32[256,256]{1,0:T(8,128)}, f32[256,256]{1,0:T(8,128)}, f32[256,256]{1,0:T(8,128)}, f32[256,256]{1,0:T(8,128)S(1)}) fusion(f32[256,256]{1,0:T(8,128)S(1)} %copy-done, f32[512,256]{1,0:T(8,128)S(1)} %copy-done.3, f32[256,256]{1,0:T(8,128)S(1)} %copy-done.4, f32[256,256]{1,0:T(8,128)S(1)} %copy-done.5), kind=kLoop, calls=%fused_computation.5 | loop fusion | flops 983040 | bytes 2359296 | tf_op jit(solution)/shard_map/sub | solution.py:39
  78.3 0.9 %copy-done.1 = f32[64,1024]{1,0:T(8,128)S(1)} copy-done((f32[64,1024]{1,0:T(8,128)S(1)}, f32[64,1024]{1,0:T(8,128)}, u32[]{:S(2)}) %copy-start.1) | copy-done | bytes 262168
  79.2 0.1 copy-done.6
  79.3 1.0 %multiply_subtract_fusion.1 = (f32[64,1024]{1,0:T(8,128)}, f32[64,1024]{1,0:T(8,128)}, f32[64,1024]{1,0:T(8,128)}) fusion(f32[64,1024]{1,0:T(8,128)S(1)} %copy-done.1, f32[64,1024]{1,0:T(8,128)S(1)} %bitcast.12, f32[64,1024]{1,0:T(8,128)S(1)} %copy-done.6, f32[64,1024]{1,0:T(8,128)S(1)} %copy-done.7), kind=kLoop, calls=%fused_computation.7 | loop fusion | flops 983040 | bytes 1835008 | tf_op jit(solution)/shard_map/sub | solution.py:39
  80.3 0.7 copy.44
  81.0 0.3 copy-done.9
  81.4 0.7 copy.45
  (20 shorter events, 0.1 us)
Async XLA Ops:
  0.7 0.7 copy-start.16
  1.5 0.6 copy-start.13
  70.0 0.7 copy-start.18
  70.0 0.7 copy-start.17
  72.1 1.0 %copy-start.8 = (f32[64,256]{1,0:T(8,128)S(1)}, f32[64,256]{1,0:T(8,128)}, u32[]{:S(2)}) copy-start(f32[64,256]{1,0:T(8,128)} %out_s.1) | copy-start | bytes 196612
  72.1 1.0 %copy-start.14 = (f32[64,256]{1,0:T(8,128)S(1)}, f32[64,256]{1,0:T(8,128)}, u32[]{:S(2)}) copy-start(f32[64,256]{1,0:T(8,128)} %param.27) | copy-start | bytes 196612
  72.1 1.0 %copy-start.15 = (f32[64,256]{1,0:T(8,128)S(1)}, f32[64,256]{1,0:T(8,128)}, u32[]{:S(2)}) copy-start(f32[64,256]{1,0:T(8,128)} %param.32) | copy-start | bytes 196612
  74.6 0.9 %copy-start.12 = (f32[64,768]{1,0:T(8,128)S(1)}, f32[64,768]{1,0:T(8,128)}, u32[]{:S(2)}) copy-start(f32[64,768]{1,0:T(8,128)} %param.31) | copy-start | bytes 589828
  74.8 1.0 %copy-start.2 = (f32[64,768]{1,0:T(8,128)S(1)}, f32[64,768]{1,0:T(8,128)}, u32[]{:S(2)}) copy-start(f32[64,768]{1,0:T(8,128)} %qkv_s.1) | copy-start | bytes 589828
  74.8 1.0 %copy-start.11 = (f32[64,768]{1,0:T(8,128)S(1)}, f32[64,768]{1,0:T(8,128)}, u32[]{:S(2)}) copy-start(f32[64,768]{1,0:T(8,128)} %param.26) | copy-start | bytes 589828
  75.8 1.0 %copy-start = (f32[256,256]{1,0:T(8,128)S(1)}, f32[256,256]{1,0:T(8,128)}, u32[]{:S(2)}) copy-start(f32[256,256]{1,0:T(8,128)} %down_s.1) | copy-start | bytes 786436
  75.8 1.3 %copy-start.3 = (f32[512,256]{1,0:T(8,128)S(1)}, f32[512,256]{1,0:T(8,128)}, u32[]{:S(2)}) copy-start(f32[512,256]{1,0:T(8,128)} %get-tuple-element.25) | copy-start | bytes 1572868
  75.8 1.4 %copy-start.4 = (f32[256,256]{1,0:T(8,128)S(1)}, f32[256,256]{1,0:T(8,128)}, u32[]{:S(2)}) copy-start(f32[256,256]{1,0:T(8,128)} %param.29) | copy-start | bytes 786436
  75.8 1.5 %copy-start.5 = (f32[256,256]{1,0:T(8,128)S(1)}, f32[256,256]{1,0:T(8,128)}, u32[]{:S(2)}) copy-start(f32[256,256]{1,0:T(8,128)} %param.34) | copy-start | bytes 786436
  77.3 1.0 %copy-start.7 = (f32[64,1024]{1,0:T(8,128)S(1)}, f32[64,1024]{1,0:T(8,128)}, u32[]{:S(2)}) copy-start(f32[64,1024]{1,0:T(8,128)} %param.33) | copy-start | bytes 786436
  78.3 0.9 %copy-start.1 = (f32[64,1024]{1,0:T(8,128)S(1)}, f32[64,1024]{1,0:T(8,128)}, u32[]{:S(2)}) copy-start(f32[64,1024]{1,0:T(8,128)} %up_s.1) | copy-start | bytes 786436
  78.3 1.0 %copy-start.6 = (f32[64,1024]{1,0:T(8,128)S(1)}, f32[64,1024]{1,0:T(8,128)}, u32[]{:S(2)}) copy-start(f32[64,1024]{1,0:T(8,128)} %param.28) | copy-start | bytes 786436
  79.3 1.0 %copy-start.10 = (bf16[512,256]{1,0:T(8,128)(2,1)S(1)}, bf16[512,256]{1,0:T(8,128)(2,1)}, u32[]{:S(2)}) copy-start(bf16[512,256]{1,0:T(8,128)(2,1)} %get-tuple-element.60) | copy-start | bytes 786436
  80.3 1.0 %copy-start.9 = (bf16[512,256]{1,0:T(8,128)(2,1)S(1)}, bf16[512,256]{1,0:T(8,128)(2,1)}, u32[]{:S(2)}) copy-start(bf16[512,256]{1,0:T(8,128)(2,1)} %get-tuple-element.61) | copy-start | bytes 786436

commit v2 on v1

--- a/solution.py
+++ b/solution.py
@@ -161,23 +161,26 @@
         self.core = 2 * self.y + 1 - self.c
         self.other = 2 * (1 - self.y) + self.c
         self.far = 2 * (1 - self.y) + 1 - self.c
+        self.x = lax.rem(self.dp, 2)
+        self.pair = self.dp + 1 - 2 * self.x
 
 
 def layer_kernel(
     n,
     lengths, tokens, cotangent, qkv_s, out_s, up_s, down_s, vec_s,
-    act_o, ig_o, ga_o, gc_o, vec_o,
+    act_o, ig_o, gd_o, gu_o, gc_o, vec_o,
     qkv_w, out_w, up_w, down_w, vec_in, vec_g, vec_z, vec_t, vec_d,
     gat_s, gat_r, vs, vr, vds, vdr,
     bias_m, q_t, k_t, v_t, do_t, o_t, dlin_t, base, dh2_s,
-    a_full, a_core, a_yo, a_yi, a_sh, a_shl, a_pc, a_tot, a_zs, a_zr, a_ds, a_dr, a_gs, a_gr,
-    c_full, c_core, c_yo, c_yi, c_sh, c_shl, c_pc, c_tot, c_zs, c_zr, c_ds, c_dr, c_gs, c_gr,
+    *groups,
 ):
     p = Place(n)
     count = tokens.shape[0]
     peers_zero = (p.core, p.other, p.far)
-    group_a = Reduction(p, a_full, a_core, a_yo, a_yi, a_sh, a_shl, a_pc, a_tot, (a_zs, a_zr, a_ds, a_dr, a_gs, a_gr))
-    group_c = Reduction(p, c_full, c_core, c_yo, c_yi, c_sh, c_shl, c_pc, c_tot, (c_zs, c_zr, c_ds, c_dr, c_gs, c_gr))
+    group_d, group_u, group_c = (
+        Reduction(p, *groups[14 * i : 14 * i + 8], groups[14 * i + 8 : 14 * i + 14]) for i in range(3)
+    )
+    d_full, u_full, c_full = group_d.full, group_u.full, group_c.full
 
     barrier = pltpu.get_barrier_semaphore()
     for peer in peers_zero:
@@ -189,32 +192,6 @@
         return carry
 
     lax.fori_loop(1, n, greet, 0)
-
-    weights = (qkv_w, out_w, up_w, down_w)
-    for buffer, shard in zip(weights, (qkv_s, out_s, up_s, down_s)):
-        buffer[p.z] = shard[...].astype(BF16)
-    pl.semaphore_wait(barrier, 3 + n - 1)
-
-    def vec_copy(i, src, dst):
-        return remote(src, dst.at[i], vs.at[i], vr.at[i], {"zero": peers_zero[i]})
-
-    def weight_copy(w, way):
-        buffer = weights[w]
-        shard = p.other if way == 2 else p.z
-        device = p.other if way == 1 else p.core
-        return remote(buffer.at[shard], buffer.at[shard], gat_s.at[w, way], gat_r.at[w, way], {"zero": device})
-
-    def weight_arrival(w, way):
-        buffer = weights[w]
-        shard = (p.core, p.other, p.far)[way]
-        device = p.other if way == 1 else p.core
-        return remote(buffer.at[shard], buffer.at[shard], gat_s.at[w, way], gat_r.at[w, way], {"zero": device})
-
-    for i in range(3):
-        vec_copy(i, vec_s, vec_in).start()
-    for w in range(4):
-        weight_copy(w, 1).start()
-        weight_copy(w, 0).start()
 
     first = lengths[0, 0]
     total = lengths[0, 0] + lengths[0, 1]
@@ -237,6 +214,55 @@
         swapped = jnp.concatenate([top[half:], top[:half]], axis=0)
         return jnp.concatenate([top * cosine + swapped * signed, lines[ROT:]], axis=0)
 
+    weights = (qkv_w, out_w, up_w, down_w)
+    for buffer, shard in zip(weights, (qkv_s, out_s, up_s, down_s)):
+        buffer[p.z] = shard[...].astype(BF16)
+    pl.semaphore_wait(barrier, 3 + n - 1)
+
+    def vec_copy(i, src, dst):
+        return remote(src, dst.at[i], vs.at[i], vr.at[i], {"zero": peers_zero[i]})
+
+    def shard_half(w, shard, half):
+        rows = weights[w].shape[1] // 2
+        return weights[w].at[shard, pl.ds(pl.multiple_of(half * rows, rows), rows)]
+
+    def weight_moves(w, way, arrival):
+        if way == 0:
+            part = weights[w].at[p.core if arrival else p.z]
+        elif way == 1:
+            part = shard_half(w, p.other if arrival else p.z, p.x)
+        elif way == 2:
+            part = shard_half(w, p.other, 1 - p.x if arrival else p.x)
+        else:
+            part = shard_half(w, p.far if arrival else p.other, p.x if way == 3 else 1 - p.x)
+        device = {1: {"zero": p.other}, 2: {"dp": p.pair}}.get(way, {"zero": p.core})
+        return remote(part, part, gat_s.at[w, way], gat_r.at[w, way], device)
+
+    def weight_copy(w, way):
+        return weight_moves(w, way, False)
+
+    def weight_arrival(w, way):
+        return weight_moves(w, way, True)
+
+    def relay_one(w):
+        weight_arrival(w, 1).wait_recv()
+        weight_copy(w, 2).start()
+        weight_copy(w, 3).start()
+
+    def relay_two(w):
+        weight_arrival(w, 2).wait_recv()
+        weight_copy(w, 4).start()
+
+    def finish_weight(w):
+        for way in (0, 3, 4):
+            weight_arrival(w, way).wait_recv()
+
+    for i in range(3):
+        vec_copy(i, vec_s, vec_in).start()
+    for w in (2, 3, 0, 1):
+        weight_copy(w, 1).start()
+        weight_copy(w, 0).start()
+
     x = tokens[...].astype(F32).T
     g = (cotangent[...].astype(F32).T * live).astype(BF16)
     centered = x - jnp.mean(x, axis=0, keepdims=True)
@@ -255,17 +281,55 @@
     h1 = (plain * gain_one + bias_one).astype(BF16)
     h2 = (plain * gain_two + bias_two).astype(BF16)
 
-    def finish_weight(w):
-        weight_arrival(w, 0).wait_recv()
-        weight_arrival(w, 2).wait_recv()
-
-    weight_arrival(0, 1).wait_recv()
-    weight_copy(0, 2).start()
-    weight_arrival(1, 1).wait_recv()
-    weight_copy(1, 2).start()
+    for w in (2, 3, 0, 1):
+        relay_one(w)
+    relay_two(2)
+    relay_two(3)
+    finish_weight(2)
+    finish_weight(3)
+
+    ones = jnp.ones((8, count), BF16)
+
+    def put_sum(at, values):
+        sums = nt(ones, values)
+        for i in range(values.shape[0] // 128):
+            vec_g[at // 128 + i : at // 128 + i + 1] = sums[0:1, 128 * i : 128 * i + 128]
+
+    def put_sum_wide(at, values):
+        high = values.astype(BF16)
+        rest = (values - high.astype(F32)).astype(BF16)
+        sums = nt(ones, high) + nt(ones, rest)
+        for i in range(values.shape[0] // 128):
+            vec_g[at // 128 + i : at // 128 + i + 1] = sums[0:1, 128 * i : 128 * i + 128]
+
+    shard_rows = W // 4
+    mlp = jnp.zeros((W, count), F32)
+    dh2 = jnp.zeros((W, count), F32)
+    for j in range(4):
+        w_up = up_w[:, :, W * j : W * j + W].reshape(W, W)
+        w_down = down_w[j]
+        up = tn(w_up, h2) + column(8 * W + W * j, W)
+        phi_sum = 0.5 + 0.5 * lax.erf(up * (0.5**0.5))
+        z = (up * phi_sum).astype(BF16)
+        bell = jnp.exp2(up * up * (-0.5 * math.log2(math.e))) * ((2.0 * math.pi) ** -0.5)
+        du = (nn(w_down, g) * (phi_sum + up * bell)).astype(BF16)
+        mlp = mlp + tn(w_down, z)
+        dh2 = dh2 + nn(w_up, du)
+        d_full[j % 2, j // 2] = nt(z, g)
+        g_up = nt(h2, du)
+        for s in range(4):
+            u_full[s % 2, s // 2, pl.ds(shard_rows * j, shard_rows)] = g_up[shard_rows * s : shard_rows * (s + 1)]
+        put_sum(8 * W + W * j, du)
+        if j == 1:
+            relay_two(0)
+            relay_two(1)
+    group_d.stage_core()
+    group_u.stage_core()
+    base[...] = x + mlp + column(12 * W, W)
+    dh2_s[...] = dh2
+
+    scale = HEAD_DIM**-0.5
     finish_weight(0)
-
-    scale = HEAD_DIM**-0.5
     for part, target in enumerate((q_t, k_t, v_t)):
         block = qkv_w[:, :, W * part : W * part + W].reshape(W, W)
         lines = tn(block, h1) + column(4 * W + W * part, W)
@@ -277,8 +341,8 @@
     finish_weight(1)
     do_t[...] = nn(out_w[...].reshape(W, W), g).astype(BF16)
 
-    weight_arrival(2, 1).wait_recv()
-    weight_copy(2, 2).start()
+    group_d.stage_y()
+    group_u.stage_y()
 
     fold = scale * math.log2(math.e)
     block = count // 2
@@ -311,51 +375,12 @@
         return carry
 
     lax.fori_loop(0, 2, head, 0)
-    weight_arrival(3, 1).wait_recv()
-    weight_copy(3, 2).start()
-    finish_weight(2)
-    finish_weight(3)
-
-    ones = jnp.ones((8, count), BF16)
-
-    def put_sum(at, values):
-        sums = nt(ones, values)
-        for i in range(values.shape[0] // 128):
-            vec_g[at // 128 + i : at // 128 + i + 1] = sums[0:1, 128 * i : 128 * i + 128]
-
-    def put_sum_wide(at, values):
-        high = values.astype(BF16)
-        rest = (values - high.astype(F32)).astype(BF16)
-        sums = nt(ones, high) + nt(ones, rest)
-        for i in range(values.shape[0] // 128):
-            vec_g[at // 128 + i : at // 128 + i + 1] = sums[0:1, 128 * i : 128 * i + 128]
-
-    shard_rows = W // 4
-    mlp = jnp.zeros((W, count), F32)
-    dh2 = jnp.zeros((W, count), F32)
-    for j in range(4):
-        w_up = up_w[:, :, W * j : W * j + W].reshape(W, W)
-        w_down = down_w[j]
-        up = tn(w_up, h2) + column(8 * W + W * j, W)
-        phi_sum = 0.5 + 0.5 * lax.erf(up * (0.5**0.5))
-        z = (up * phi_sum).astype(BF16)
-        bell = jnp.exp2(up * up * (-0.5 * math.log2(math.e))) * ((2.0 * math.pi) ** -0.5)
-        du = (nn(w_down, g) * (phi_sum + up * bell)).astype(BF16)
-        mlp = mlp + tn(w_down, z)
-        dh2 = dh2 + nn(w_up, du)
-        a_full[j % 2, j // 2, pl.ds(0, W)] = nt(z, g)
-        g_up = nt(h2, du)
-        for s in range(4):
-            a_full[s % 2, s // 2, pl.ds(W + shard_rows * j, shard_rows)] = g_up[shard_rows * s : shard_rows * (s + 1)]
-        put_sum(8 * W + W * j, du)
-    group_a.stage_core()
-    base[...] = x + mlp + column(12 * W, W)
-    dh2_s[...] = dh2
-
+    group_d.stage_scatter()
     lax.fori_loop(2, 4, head, 0)
-    group_a.stage_y()
+    group_u.stage_scatter()
+    group_d.stage_gather()
     lax.fori_loop(4, 6, head, 0)
-    group_a.stage_scatter()
+    group_u.stage_gather()
     lax.fori_loop(6, 8, head, 0)
 
     for j in range(3):
@@ -368,7 +393,6 @@
     for s in range(4):
         c_full[s % 2, s // 2, pl.ds(3 * shard_rows, shard_rows)] = g_out[shard_rows * s : shard_rows * (s + 1)]
     group_c.stage_core()
-    group_a.stage_gather()
 
     dh1 = jnp.zeros((W, count), F32)
     for j in range(3):
@@ -407,20 +431,23 @@
     act_o[...] = ((base[...] + attn) * live).T.astype(BF16)
 
     group_c.stage_gather()
-    group_a.stage_end()
-    ga_o[...] = a_tot[...].astype(F32)
+    group_d.stage_end()
+    gd_o[...] = group_d.total[...]
+    group_u.stage_end()
+    gu_o[...] = group_u.total[...]
     group_c.loop(lambda k: vec_dp(k).wait_recv())
     vec_o[...] = lax.fori_loop(1, n, lambda k, s: s + vec_d[k], vec_t[...])
     for w in range(4):
-        for way in range(3):
+        for way in range(5):
             weight_copy(w, way).wait_send()
     for i in range(3):
         vec_copy(i, vec_s, vec_in).wait_send()
         vec_zero(i).wait_send()
     group_c.loop(lambda k: vec_dp(k).wait_send())
-    group_a.drain()
+    group_d.drain()
+    group_u.drain()
     group_c.stage_end()
-    gc_o[...] = c_tot[...].astype(F32)
+    gc_o[...] = group_c.total[...]
     group_c.drain()
 
 
@@ -447,20 +474,20 @@
 def layer(n, lengths, tokens, cotangent, qkv, out, up, down, vec):
     count = tokens.shape[0]
     dma = pltpu.SemaphoreType.DMA
-    a_rows = n * piece_rows(512, n)
-    c_rows = n * piece_rows(256, n)
+    rows = n * piece_rows(256, n)
     vmem = pl.BlockSpec(memory_space=pltpu.VMEM)
     return pl.pallas_call(
         functools.partial(layer_kernel, n),
         out_shape=(
             jax.ShapeDtypeStruct(tokens.shape, BF16),
             jax.ShapeDtypeStruct(tokens.shape, BF16),
-            jax.ShapeDtypeStruct((a_rows, W), F32),
-            jax.ShapeDtypeStruct((c_rows, W), F32),
+            jax.ShapeDtypeStruct((rows, W), BF16),
+            jax.ShapeDtypeStruct((rows, W), BF16),
+            jax.ShapeDtypeStruct((rows, W), BF16),
             jax.ShapeDtypeStruct((VROWS, 128), F32),
         ),
         in_specs=[pl.BlockSpec(memory_space=pltpu.SMEM)] + [vmem] * 7,
-        out_specs=[vmem] * 5,
+        out_specs=[vmem] * 6,
         scratch_shapes=[
             pltpu.VMEM((4, 64, 3 * W), BF16),
             pltpu.VMEM((4, 64, W), BF16),
@@ -471,7 +498,7 @@
             pltpu.VMEM((3, VROWS, 128), F32),
             pltpu.VMEM((VROWS, 128), F32),
             pltpu.VMEM((n, VROWS, 128), F32),
-            dma((4, 3)), dma((4, 3)), dma((6,)), dma((6,)), dma((n,)), dma((n,)),
+            dma((4, 5)), dma((4, 5)), dma((6,)), dma((6,)), dma((n,)), dma((n,)),
             pltpu.VMEM((count, count), F32),
             pltpu.VMEM((W, count), BF16),
             pltpu.VMEM((W, count), BF16),
@@ -482,13 +509,75 @@
             pltpu.VMEM((W, count), F32),
             pltpu.VMEM((W, count), F32),
         ]
-        + reduction_scratch(512, n, F32)
-        + reduction_scratch(256, n, F32),
+        + reduction_scratch(W, n, BF16) * 3,
         compiler_params=pltpu.CompilerParams(
             collective_id=0, has_side_effects=True, vmem_limit_bytes=56 * 1024 * 1024
         ),
         name="layer",
     )(lengths, tokens, cotangent, qkv, out, up, down, vec)
+
+
+RATES = (RATE_MATRIX, RATE_OUTPUT, RATE_MATRIX, RATE_MATRIX)
+
+
+def update_kernel(*refs):
+    passed, sums, states = refs[0:2], refs[2:5], refs[5:17]
+    passed_o, states_o = refs[17:19], refs[19:31]
+    sums_v, ins, outs = refs[31:34], refs[34:46], refs[46:58]
+    held = refs[58:60]
+    pass_sem, sum_sem, in_sem, out_sem = refs[60:64]
+    order = (3, 2, 0, 1)
+    through_in = [pltpu.make_async_copy(passed[i], held[i], pass_sem.at[i]) for i in range(2)]
+    through = [pltpu.make_async_copy(held[i], passed_o[i], pass_sem.at[2 + i]) for i in range(2)]
+    sum_in = [pltpu.make_async_copy(sums[i], sums_v[i], sum_sem.at[i]) for i in range(3)]
+    copy_in = [pltpu.make_async_copy(states[i], ins[i], in_sem.at[i]) for i in range(12)]
+    copy_out = [pltpu.make_async_copy(outs[i], states_o[i], out_sem.at[i]) for i in range(12)]
+    for copy in sum_in:
+        copy.start()
+    for w in order:
+        for kind in range(3):
+            copy_in[4 * kind + w].start()
+    for copy in through_in:
+        copy.start()
+    for copy in sum_in:
+        copy.wait()
+    quarter = W // 4
+    for w in order:
+        if w == 2:
+            for i in range(2):
+                through_in[i].wait()
+                through[i].start()
+        for kind in range(3):
+            copy_in[4 * kind + w].wait()
+        rows, columns = ins[w].shape
+        begin = (0, 3 * quarter, 0, 0)[w]
+        group = sums_v[(2, 2, 1, 0)[w]]
+        for j in range(columns // W):
+            cut = slice(W * j, W * j + W)
+            grad = group[begin + rows * j : begin + rows * j + rows].astype(F32)
+            new = adamw(ins[w][:, cut], ins[4 + w][:, cut], ins[8 + w][:, cut], grad, RATES[w])
+            for kind in range(3):
+                outs[4 * kind + w][:, cut] = new[kind]
+        for kind in range(3):
+            copy_out[4 * kind + w].start()
+    for copy in copy_out + through:
+        copy.wait()
+
+
+def update(activations, input_grad, sums, states):
+    hbm = pl.BlockSpec(memory_space=pl.ANY)
+    shapes = [jax.ShapeDtypeStruct(a.shape, a.dtype) for a in (activations, input_grad) + states]
+    dma = pltpu.SemaphoreType.DMA
+    return pl.pallas_call(
+        update_kernel,
+        out_shape=shapes,
+        in_specs=[hbm] * 17,
+        out_specs=[hbm] * 14,
+        scratch_shapes=[pltpu.VMEM(a.shape, a.dtype) for a in sums + states + states + (activations, input_grad)]
+        + [dma((4,)), dma((3,)), dma((12,)), dma((12,))],
+        compiler_params=pltpu.CompilerParams(vmem_limit_bytes=56 * 1024 * 1024),
+        name="update",
+    )(activations, input_grad, *sums, *states)
 
 
 def on_device(
@@ -515,21 +604,20 @@
     share = vectors.shape[0]
     begin = lax.axis_index("zero") * share
     vec = lax.dynamic_update_slice(jnp.zeros((VROWS * 128,), F32), vectors, (begin,)).reshape(VROWS, 128)
-    activations, input_grad, sum_a, sum_c, sum_vec = layer(
+    activations, input_grad, *sums, sum_vec = layer(
         n, lengths, tokens, cotangent, qkv_weight, out_weight, up_weight, down_weight, vec
     )
-    down_sum = sum_a[:W]
-    up_sum = sum_a[W : 2 * W].reshape(4, W // 4, W).transpose(1, 0, 2).reshape(W // 4, 4 * W)
-    qkv_sum = sum_c[: 3 * W // 4].reshape(3, W // 4, W).transpose(1, 0, 2).reshape(W // 4, 3 * W)
-    out_sum = sum_c[3 * W // 4 : W]
     vec_sum = lax.dynamic_slice(sum_vec.reshape(-1), (begin,), (share,))
-    qkv_new = adamw(qkv_weight, qkv_first, qkv_second, qkv_sum, RATE_MATRIX)
-    out_new = adamw(out_weight, out_first, out_second, out_sum, RATE_OUTPUT)
-    up_new = adamw(up_weight, up_first, up_second, up_sum, RATE_MATRIX)
-    down_new = adamw(down_weight, down_first, down_second, down_sum, RATE_MATRIX)
     vec_new = adamw(vectors, vectors_first, vectors_second, vec_sum, RATE_VECTOR)
-    news = (qkv_new, out_new, up_new, down_new, vec_new)
-    return (activations, input_grad) + tuple(new[i] for i in range(3) for new in news)
+    states = (
+        qkv_weight, out_weight, up_weight, down_weight,
+        qkv_first, out_first, up_first, down_first,
+        qkv_second, out_second, up_second, down_second,
+    )
+    news = update(activations, input_grad, tuple(sums), states)
+    return (
+        *news[0:6], vec_new[0], *news[6:10], vec_new[1], *news[10:14], vec_new[2],
+    )
 
 
 def solution(mesh):

time: 82.5 us -> 68.6 us (0.83)
  local copies, waits for them, and re-layouts: 7.62 us -> 2.13 us
  other arithmetic: 5.81 us -> 1.39 us
  Pallas kernels: 67.8 us -> 64 us
    pallas_call x1, Pallas kernels: 67.8 us -> 60.2 us  [layer(): pl.pallas_call(functools.partial(layer_kernel, n), out_shape=(jax.ShapeDt...]
    sub x5 -> x1, other arithmetic: 5.81 us -> 1.39 us  [adamw(): return (master - rate * (direction + DECAY * master), momentum, variance)]
    unnamed x41 -> x8, local copies, waits for them, and re-layouts: 6.32 us -> 1.96 us
    pallas_call x0 -> x1, Pallas kernels: none -> 3.8 us  [update(): pl.pallas_call(update_kernel, out_shape=shapes, in_specs=[hbm] * 17, out_...]
    slice x1 -> x0, local copies, waits for them, and re-layouts: 0.98 us -> none  [on_device(): sum_c[:3 * W // 4].reshape(3, W // 4, W).transpose(1, 0, 2)]
where the time goes in v2:
time: 68.6 us; the launch traced here: 68.3 us
  Pallas kernels  64 us (93%)
  local copies, waits for them, and re-layouts  2.13 us (3%)
  other arithmetic  1.39 us (2%)
  between operations  0.7 us (1%)
    pallas_call x1, Pallas kernels, layer(): pl.pallas_call(functools.partial(layer_kernel, n), out_shape=(jax.ShapeDt...  60.2 us
    pallas_call x1, Pallas kernels, update(): pl.pallas_call(update_kernel, out_shape=shapes, in_specs=[hbm] * 17, out_...  3.8 us
    unnamed x8, local copies, waits for them, and re-layouts  1.96 us
    sub x1, other arithmetic, adamw(): return (master - rate * (direction + DECAY * master), momentum, variance)  1.39 us

profile of v2, /device:TPU:0, one launch (start us, length us, event | category | flops | bytes accessed | tf_op | source)
XLA Modules:
  0.0 68.3 jit_solution(4329268152707665670)
XLA Ops:
  0.7 0.0 copy-start.1
  0.7 0.7 copy-done.1
  1.3 0.2 dynamic_update_slice.3
  1.5 0.0 copy-start
  1.5 0.6 copy-done
  2.1 60.2 %layer.1 = (bf16[512,256]{1,0:T(8,128)(2,1)}, bf16[512,256]{1,0:T(8,128)(2,1)}, bf16[256,256]{1,0:T(8,128)(2,1)}, bf16[256,256]{1,0:T(8,128)(2,1)}, bf16[256,256]{1,0:T(8,128)(2,1)}, /*index=5*/f32[32,128]{1,0:T(8,128)}) custom-call(s32[1,2]{1,0:T(1,128)} %lengths.1, bf16[512,256]{1,0:T(8,128)(2,1)} %tokens.1, bf16[512,256]{1,0:T(8,128)(2,1)} %cotangent.1, ...), custom_call_target="tpu_custom_call" | custom-call | tf_op jit(solution)/shard_map/layer/pallas_call | solution.py:479
  62.4 0.0 copy-start.3
  62.4 0.0 copy-start.2
  62.4 0.7 copy-done.3
  63.1 0.0 copy-done.2
  63.1 1.4 %multiply_subtract_fusion = (f32[832]{0:T(1024)}, f32[832]{0:T(1024)}, f32[832]{0:T(1024)}) fusion(f32[832]{0:T(1024)S(1)} %copy-done.1, f32[4096]{0:T(1024)} %bitcast.3, s32[]{:T(128)S(6)} %select_n.4, f32[832]{0:T(1024)S(1)} %copy-done.2, f32[832]{0:T(1024)S(1)} %copy-done.3), kind=kLoop, calls=%fused_computation.2 | loop fusion | flops 12480 | bytes 23300 | tf_op jit(solution)/shard_map/sub | solution.py:39
  64.5 3.8 %update.1 = (bf16[512,256]{1,0:T(8,128)(2,1)}, bf16[512,256]{1,0:T(8,128)(2,1)}, f32[64,768]{1,0:T(8,128)}, f32[64,256]{1,0:T(8,128)}, f32[64,1024]{1,0:T(8,128)...) custom-call(bf16[512,256]{1,0:T(8,128)(2,1)} %get-tuple-element.37.r, ...), custom_call_target="tpu_custom_call" | custom-call | tf_op jit(solution)/shard_map/update/pallas_call | solution.py:571
  (1 shorter events, 0.0 us)
Async XLA Ops:
  0.7 0.7 %copy-start.1 = (f32[832]{0:T(1024)S(1)}, f32[832]{0:T(1024)}, u32[]{:S(2)}) copy-start(f32[832]{0:T(1024)} %param.25) | copy-start | bytes 9988
  1.5 0.6 copy-start
  62.4 0.7 %copy-start.3 = (f32[832]{0:T(1024)S(1)}, f32[832]{0:T(1024)}, u32[]{:S(2)}) copy-start(f32[832]{0:T(1024)} %param.35) | copy-start | bytes 9988
  62.4 0.7 %copy-start.2 = (f32[832]{0:T(1024)S(1)}, f32[832]{0:T(1024)}, u32[]{:S(2)}) copy-start(f32[832]{0:T(1024)} %param.30) | copy-start | bytes 9988

commit v3 on v2

--- a/solution.py
+++ b/solution.py
@@ -222,7 +222,11 @@
     def vec_copy(i, src, dst):
         return remote(src, dst.at[i], vs.at[i], vr.at[i], {"zero": peers_zero[i]})
 
+    ways = ((0, 1, 3), (0, 1, 3), (0, 1, 2, 3, 4), (0, 1, 2, 3, 4))
+
     def shard_half(w, shard, half):
+        if w < 2:
+            return weights[w].at[shard]
         rows = weights[w].shape[1] // 2
         return weights[w].at[shard, pl.ds(pl.multiple_of(half * rows, rows), rows)]
 
@@ -246,7 +250,8 @@
 
     def relay_one(w):
         weight_arrival(w, 1).wait_recv()
-        weight_copy(w, 2).start()
+        if w >= 2:
+            weight_copy(w, 2).start()
         weight_copy(w, 3).start()
 
     def relay_two(w):
@@ -254,12 +259,13 @@
         weight_copy(w, 4).start()
 
     def finish_weight(w):
-        for way in (0, 3, 4):
-            weight_arrival(w, way).wait_recv()
+        for way in ways[w]:
+            if way in (0, 3, 4):
+                weight_arrival(w, way).wait_recv()
 
     for i in range(3):
         vec_copy(i, vec_s, vec_in).start()
-    for w in (2, 3, 0, 1):
+    for w in range(2):
         weight_copy(w, 1).start()
         weight_copy(w, 0).start()
 
@@ -281,52 +287,11 @@
     h1 = (plain * gain_one + bias_one).astype(BF16)
     h2 = (plain * gain_two + bias_two).astype(BF16)
 
-    for w in (2, 3, 0, 1):
-        relay_one(w)
-    relay_two(2)
-    relay_two(3)
-    finish_weight(2)
-    finish_weight(3)
-
-    ones = jnp.ones((8, count), BF16)
-
-    def put_sum(at, values):
-        sums = nt(ones, values)
-        for i in range(values.shape[0] // 128):
-            vec_g[at // 128 + i : at // 128 + i + 1] = sums[0:1, 128 * i : 128 * i + 128]
-
-    def put_sum_wide(at, values):
-        high = values.astype(BF16)
-        rest = (values - high.astype(F32)).astype(BF16)
-        sums = nt(ones, high) + nt(ones, rest)
-        for i in range(values.shape[0] // 128):
-            vec_g[at // 128 + i : at // 128 + i + 1] = sums[0:1, 128 * i : 128 * i + 128]
-
-    shard_rows = W // 4
-    mlp = jnp.zeros((W, count), F32)
-    dh2 = jnp.zeros((W, count), F32)
-    for j in range(4):
-        w_up = up_w[:, :, W * j : W * j + W].reshape(W, W)
-        w_down = down_w[j]
-        up = tn(w_up, h2) + column(8 * W + W * j, W)
-        phi_sum = 0.5 + 0.5 * lax.erf(up * (0.5**0.5))
-        z = (up * phi_sum).astype(BF16)
-        bell = jnp.exp2(up * up * (-0.5 * math.log2(math.e))) * ((2.0 * math.pi) ** -0.5)
-        du = (nn(w_down, g) * (phi_sum + up * bell)).astype(BF16)
-        mlp = mlp + tn(w_down, z)
-        dh2 = dh2 + nn(w_up, du)
-        d_full[j % 2, j // 2] = nt(z, g)
-        g_up = nt(h2, du)
-        for s in range(4):
-            u_full[s % 2, s // 2, pl.ds(shard_rows * j, shard_rows)] = g_up[shard_rows * s : shard_rows * (s + 1)]
-        put_sum(8 * W + W * j, du)
-        if j == 1:
-            relay_two(0)
-            relay_two(1)
-    group_d.stage_core()
-    group_u.stage_core()
-    base[...] = x + mlp + column(12 * W, W)
-    dh2_s[...] = dh2
+    relay_one(0)
+    relay_one(1)
+    for w in (2, 3):
+        weight_copy(w, 1).start()
+        weight_copy(w, 0).start()
 
     scale = HEAD_DIM**-0.5
     finish_weight(0)
@@ -340,9 +305,6 @@
             target[HEAD_DIM * h : HEAD_DIM * h + HEAD_DIM] = piece.astype(BF16)
     finish_weight(1)
     do_t[...] = nn(out_w[...].reshape(W, W), g).astype(BF16)
-
-    group_d.stage_y()
-    group_u.stage_y()
 
     fold = scale * math.log2(math.e)
     block = count // 2
@@ -374,14 +336,59 @@
         dlin_t[2, at] = dv.astype(BF16)
         return carry
 
-    lax.fori_loop(0, 2, head, 0)
+    relay_one(2)
+    relay_one(3)
+    lax.fori_loop(0, 2, head, 0, unroll=True)
+    relay_two(2)
+    relay_two(3)
+    lax.fori_loop(2, 4, head, 0, unroll=True)
+    finish_weight(2)
+    finish_weight(3)
+
+    ones = jnp.ones((8, count), BF16)
+
+    def put_sum(at, values):
+        sums = nt(ones, values)
+        for i in range(values.shape[0] // 128):
+            vec_g[at // 128 + i : at // 128 + i + 1] = sums[0:1, 128 * i : 128 * i + 128]
+
+    def put_sum_wide(at, values):
+        high = values.astype(BF16)
+        rest = (values - high.astype(F32)).astype(BF16)
+        sums = nt(ones, high) + nt(ones, rest)
+        for i in range(values.shape[0] // 128):
+            vec_g[at // 128 + i : at // 128 + i + 1] = sums[0:1, 128 * i : 128 * i + 128]
+
+    shard_rows = W // 4
+    mlp = jnp.zeros((W, count), F32)
+    dh2 = jnp.zeros((W, count), F32)
+    for j in range(4):
+        w_up = up_w[:, :, W * j : W * j + W].reshape(W, W)
+        w_down = down_w[j]
+        up = tn(w_up, h2) + column(8 * W + W * j, W)
+        phi_sum = 0.5 + 0.5 * lax.erf(up * (0.5**0.5))
+        z = (up * phi_sum).astype(BF16)
+        bell = jnp.exp2(up * up * (-0.5 * math.log2(math.e))) * ((2.0 * math.pi) ** -0.5)
+        du = (nn(w_down, g) * (phi_sum + up * bell)).astype(BF16)
+        mlp = mlp + tn(w_down, z)
+        dh2 = dh2 + nn(w_up, du)
+        d_full[j % 2, j // 2] = nt(z, g)
+        g_up = nt(h2, du)
+        for s in range(4):
+            u_full[s % 2, s // 2, pl.ds(shard_rows * j, shard_rows)] = g_up[shard_rows * s : shard_rows * (s + 1)]
+        put_sum(8 * W + W * j, du)
+    group_d.stage_core()
+    group_u.stage_core()
+    base[...] = x + mlp + column(12 * W, W)
+    dh2_s[...] = dh2
+    group_d.stage_y()
+    group_u.stage_y()
+
+    lax.fori_loop(4, 6, head, 0, unroll=True)
     group_d.stage_scatter()
-    lax.fori_loop(2, 4, head, 0)
     group_u.stage_scatter()
+    lax.fori_loop(6, 8, head, 0, unroll=True)
     group_d.stage_gather()
-    lax.fori_loop(4, 6, head, 0)
-    group_u.stage_gather()
-    lax.fori_loop(6, 8, head, 0)
 
     for j in range(3):
         dlin = dlin_t[j]
@@ -393,6 +400,7 @@
     for s in range(4):
         c_full[s % 2, s // 2, pl.ds(3 * shard_rows, shard_rows)] = g_out[shard_rows * s : shard_rows * (s + 1)]
     group_c.stage_core()
+    group_u.stage_gather()
 
     dh1 = jnp.zeros((W, count), F32)
     for j in range(3):
@@ -438,7 +446,7 @@
     group_c.loop(lambda k: vec_dp(k).wait_recv())
     vec_o[...] = lax.fori_loop(1, n, lambda k, s: s + vec_d[k], vec_t[...])
     for w in range(4):
-        for way in range(5):
+        for way in ways[w]:
             weight_copy(w, way).wait_send()
     for i in range(3):
         vec_copy(i, vec_s, vec_in).wait_send()

time: 68.6 us -> 66 us (0.962)
  Pallas kernels: 64 us -> 61.2 us
    pallas_call x1, Pallas kernels: 60.2 us -> 57.4 us  [layer(): pl.pallas_call(functools.partial(layer_kernel, n), out_shape=(jax.ShapeDt...]
where the time goes in v3:
time: 66 us; the launch traced here: 65.6 us
  Pallas kernels  61.2 us (93%)
  local copies, waits for them, and re-layouts  2.13 us (3%)
  other arithmetic  1.39 us (2%)
  between operations  0.86 us (1%)
    pallas_call x1, Pallas kernels, layer(): pl.pallas_call(functools.partial(layer_kernel, n), out_shape=(jax.ShapeDt...  57.4 us
    pallas_call x1, Pallas kernels, update(): pl.pallas_call(update_kernel, out_shape=shapes, in_specs=[hbm] * 17, out_...  3.8 us
    unnamed x8, local copies, waits for them, and re-layouts  1.96 us
    sub x1, other arithmetic, adamw(): return (master - rate * (direction + DECAY * master), momentum, variance)  1.39 us

profile of v3, /device:TPU:0, one launch (start us, length us, event | category | flops | bytes accessed | tf_op | source)
XLA Modules:
  0.0 65.6 jit_solution(11162118475837270601)
XLA Ops:
  0.7 0.0 copy-start.1
  0.7 0.7 %copy-done.1 = f32[832]{0:T(1024)S(1)} copy-done((f32[832]{0:T(1024)S(1)}, f32[832]{0:T(1024)}, u32[]{:S(2)}) %copy-start.1) | copy-done | bytes 3352
  1.3 0.2 dynamic_update_slice.3
  1.5 0.0 copy-start
  1.5 0.6 copy-done
  2.1 57.4 %layer.1 = (bf16[512,256]{1,0:T(8,128)(2,1)}, bf16[512,256]{1,0:T(8,128)(2,1)}, bf16[256,256]{1,0:T(8,128)(2,1)}, bf16[256,256]{1,0:T(8,128)(2,1)}, bf16[256,256]{1,0:T(8,128)(2,1)}, /*index=5*/f32[32,128]{1,0:T(8,128)}) custom-call(s32[1,2]{1,0:T(1,128)} %lengths.1, bf16[512,256]{1,0:T(8,128)(2,1)} %tokens.1, bf16[512,256]{1,0:T(8,128)(2,1)} %cotangent.1, ...), custom_call_target="tpu_custom_call" | custom-call | tf_op jit(solution)/shard_map/layer/pallas_call | solution.py:487
  59.6 0.0 copy-start.3
  59.6 0.0 copy-start.2
  59.6 0.7 %copy-done.3 = f32[832]{0:T(1024)S(1)} copy-done((f32[832]{0:T(1024)S(1)}, f32[832]{0:T(1024)}, u32[]{:S(2)}) %copy-start.3) | copy-done | bytes 3352
  60.2 0.0 copy-done.2
  60.3 1.4 %multiply_subtract_fusion = (f32[832]{0:T(1024)}, f32[832]{0:T(1024)}, f32[832]{0:T(1024)}) fusion(f32[832]{0:T(1024)S(1)} %copy-done.1, f32[4096]{0:T(1024)} %bitcast.3, s32[]{:T(128)S(6)} %select_n.4, f32[832]{0:T(1024)S(1)} %copy-done.2, f32[832]{0:T(1024)S(1)} %copy-done.3), kind=kLoop, calls=%fused_computation.2 | loop fusion | flops 12480 | bytes 23300 | tf_op jit(solution)/shard_map/sub | solution.py:39
  61.6 3.8 %update.1 = (bf16[512,256]{1,0:T(8,128)(2,1)}, bf16[512,256]{1,0:T(8,128)(2,1)}, f32[64,768]{1,0:T(8,128)}, f32[64,256]{1,0:T(8,128)}, f32[64,1024]{1,0:T(8,128)...) custom-call(bf16[512,256]{1,0:T(8,128)(2,1)} %get-tuple-element.37.r, ...), custom_call_target="tpu_custom_call" | custom-call | tf_op jit(solution)/shard_map/update/pallas_call | solution.py:579
  (1 shorter events, 0.0 us)
Async XLA Ops:
  0.7 0.7 %copy-start.1 = (f32[832]{0:T(1024)S(1)}, f32[832]{0:T(1024)}, u32[]{:S(2)}) copy-start(f32[832]{0:T(1024)} %param.25) | copy-start | bytes 9988
  1.5 0.6 copy-start
  59.6 0.7 %copy-start.3 = (f32[832]{0:T(1024)S(1)}, f32[832]{0:T(1024)}, u32[]{:S(2)}) copy-start(f32[832]{0:T(1024)} %param.35) | copy-start | bytes 9988
  59.6 0.7 %copy-start.2 = (f32[832]{0:T(1024)S(1)}, f32[832]{0:T(1024)}, u32[]{:S(2)}) copy-start(f32[832]{0:T(1024)} %param.30) | copy-start | bytes 9988
